TPU v7x, 256 devices: a whole 4x4x8 slice. The times are simulated.
256 devices in a mesh: expert: 8 (over y, core), row: 8 (over z), col: 4 (over x).
Axes of the slice: x: 4, y: 4, z: 8, core: 2. Of those that a mesh axis runs over, the one named last changes fastest.
Arguments:
- tokens_grad: bfloat16 [1536, 3072], P('expert', ('row', 'col')), may hold values from -2.390625 to 2.390625
- expert_ids: int32 [1536, 2], P('expert'), may hold values from 0 to 7, all different within a row; in each aligned block of 192 rows (0 to 191, 192 to 383, ...) at most 72 rows name the same one
- combine_weights: float32 [1536, 2], P('expert'), may hold values from 0.1 to 1
- gate_saved: bfloat16 [8, 576, 16384], P('expert', None, ('row', 'col')), may hold values from -9 to 9
- up_saved: bfloat16 [8, 576, 16384], P('expert', None, ('row', 'col')), may hold values from -6 to 6
- gate_weight: bfloat16 [8, 3072, 16384], P('expert', None, ('row', 'col')), may hold values from -0.21875 to 0.21875
- up_weight: bfloat16 [8, 3072, 16384], P('expert', None, ('row', 'col')), may hold values from -0.109375 to 0.109375
- down_weight: bfloat16 [8, 16384, 3072], P('expert', ('row', 'col')), may hold values from -0.046875 to 0.046875
Outputs:
- tokens_input_grad: bfloat16 [1536, 3072], P('expert', ('row', 'col'))
Inputs may be any that keep to these rules, and one draw needn't show every extreme that they name: `expert_ids`: each token names 2 different experts. Among the 192 tokens of one group no expert is named more than 72 times, and in every draw some group names some expert exactly 72 times.
All inputs are finite; a program needn't handle non-finite values.
Results may differ from a plain program's by a relative error of at most 0.0065.
Values may be sent and summed in bfloat16 or wider, within the bound.
A program may use at most 64 MiB of HBM per device.

v0:
```python
import jax
import jax.numpy as jnp
from jax import lax
from jax.sharding import PartitionSpec as P

tanh_scale = 0.7978845608028654
cubic_term = 0.044715


def gelu_pair(pre_act):
    inner_arg = tanh_scale * (pre_act + cubic_term * pre_act * pre_act * pre_act)
    tanh_part = jnp.tanh(inner_arg)
    activation = 0.5 * pre_act * (1.0 + tanh_part)
    derivative = 0.5 * (1.0 + tanh_part) + 0.5 * pre_act * (
        1.0 - tanh_part * tanh_part
    ) * tanh_scale * (1.0 + 3.0 * cubic_term * pre_act * pre_act)
    return (activation, derivative)


def local_slots(expert_ids, experts, capacity):
    flat_ids = expert_ids.reshape(-1)
    onehot = (flat_ids[:, None] == jnp.arange(experts, dtype=jnp.int32)[None, :]).astype(jnp.int32)
    earlier = jnp.cumsum(onehot, axis=0) - onehot
    position = jnp.sum(earlier * onehot, axis=1)
    return flat_ids * capacity + position


def per_device(
    tokens_grad,
    expert_ids,
    combine_weights,
    gate_saved,
    up_saved,
    gate_weight,
    up_weight,
    down_weight,
):
    experts = lax.axis_size("expert")
    slot_count = gate_saved.shape[1]
    capacity = slot_count // experts
    tok_count, top_count = expert_ids.shape
    feat_local = tokens_grad.shape[1]
    gate_rows = gate_saved[0]
    up_rows = up_saved[0]
    gate_mat = gate_weight[0]
    up_mat = up_weight[0]
    down_mat = down_weight[0]
    slot_index = local_slots(expert_ids, experts, capacity)
    slot_range = jnp.arange(slot_count, dtype=jnp.int32)
    dispatch = (slot_index[None, :] == slot_range[:, None]).astype(jnp.bfloat16)
    pair_hits = slot_index.reshape(tok_count, top_count)[:, :, None] == slot_range[None, None, :]
    combine = jnp.sum(pair_hits.astype(jnp.float32), axis=1).astype(jnp.bfloat16)
    scaled = (combine_weights[:, :, None] * tokens_grad.astype(jnp.float32)[:, None, :]).astype(
        jnp.bfloat16
    )
    scaled = scaled.reshape(tok_count * top_count, feat_local)
    outgoing = jnp.dot(dispatch, scaled, preferred_element_type=jnp.float32).astype(jnp.bfloat16)
    outgoing = outgoing.reshape(experts, capacity, feat_local)
    activation, derivative = gelu_pair(gate_rows.astype(jnp.float32))
    up_float = up_rows.astype(jnp.float32)
    routed = lax.all_to_all(outgoing, "expert", split_axis=0, concat_axis=0, tiled=True).reshape(
        slot_count, feat_local
    )
    hidden_grad = lax.dot_general(
        lax.all_gather(routed, ("row", "col"), axis=1, tiled=True),
        down_mat,
        (((1,), (1,)), ((), ())),
        preferred_element_type=jnp.float32,
    )
    gate_grad = (hidden_grad * up_float * derivative).astype(jnp.bfloat16)
    up_grad = (hidden_grad * activation).astype(jnp.bfloat16)
    gate_term = lax.dot_general(
        gate_grad, gate_mat, (((1,), (1,)), ((), ())), preferred_element_type=jnp.float32
    )
    up_term = lax.dot_general(
        up_grad, up_mat, (((1,), (1,)), ((), ())), preferred_element_type=jnp.float32
    )
    summed = lax.psum_scatter(gate_term + up_term, ("row", "col"), scatter_dimension=1, tiled=True)
    slot_grad = summed.astype(jnp.bfloat16)
    arrived = lax.all_to_all(
        slot_grad.reshape(experts, capacity, feat_local),
        "expert",
        split_axis=0,
        concat_axis=0,
        tiled=True,
    )
    arrived = arrived.reshape(slot_count, feat_local)
    return jnp.dot(combine, arrived, preferred_element_type=jnp.float32).astype(jnp.bfloat16)


def solution(mesh):
    in_specs = (
        P("expert", ("row", "col")),
        P("expert", None),
        P("expert", None),
        P("expert", None, ("row", "col")),
        P("expert", None, ("row", "col")),
        P("expert", None, ("row", "col")),
        P("expert", None, ("row", "col")),
        P("expert", ("row", "col"), None),
    )
    out_specs = P("expert", ("row", "col"))
    return jax.shard_map(
        per_device, mesh=mesh, in_specs=in_specs, out_specs=out_specs, check_vma=False
    )
```

profile of v0, /device:TPU:1, one launch (start us, length us, event | category | flops | bytes accessed | tf_op | source)
XLA Modules:
  0.0 365.0 jit_solution(15090732196982929019)
XLA Ops:
  6.5 0.0 copy-start
  6.5 0.0 all-gather.2.cloned.1.call-start
  6.5 0.9 copy.34
  7.5 0.1 eq.55
  7.6 0.1 eq.51
  7.8 0.9 reduce-window.6
  8.7 0.2 slice_reduce_fusion
  8.9 0.1 fusion.35
  9.0 0.8 copy.37
  9.8 0.1 mul.97
  10.0 0.9 mul.99
  10.8 0.3 convolution_convert_fusion
  11.2 0.1 copy.38
  11.3 11.2 %all_to_all.10 = bf16[8,72,96]{2,1,0:T(8,128)(2,1)S(1)} all-to-all(bf16[8,72,96]{2,1,0:T(8,128)(2,1)S(1)} %bitcast.43), channel_id=1, replica_groups=mesh['expert'=8,'row'=8,'col'=4] {'expert'}, dimensions={0} | all-to-all | bytes 221184 | tf_op jit(solution)/shard_map/all_to_all | solution.py:61
  22.5 0.8 copy.39
  23.3 0.0 all-gather.2.cloned.1.call-update
  23.3 0.0 reduce-scatter.2.cloned.1.call-start
  23.4 79.7 %all-gather.2.cloned.1.call-done = bf16[576,3072]{0,1:T(8,128)(2,1)} async-done(((bf16[576,96]{0,1:T(8,128)(2,1)}), bf16[576,3072]{0,1:T(8,128)(2,1)}) %all-gather.2.cloned.1.call-update) | async-done | bytes 3538960 | tf_op jit(solution)/shard_map/all_gather | solution.py:65
  103.1 0.0 copy-start.2
  103.1 0.0 copy-start.4
  103.1 5.6 %fusion.3 = f32[576,512]{1,0:T(8,128)S(1)} fusion(bf16[576,3072]{0,1:T(8,128)(2,1)} %all-gather.2.cloned.1.call-done, bf16[1,512,3072]{2,1,0:T(8,128)(2,1)} %param.15), kind=kOutput, calls=%fused_computation.4 | convolution fusion | flops 1811939328 | bytes 7864320 | tf_op jit(solution)/shard_map/dot_general | solution.py:64
  108.6 0.0 copy-done
  108.6 0.0 copy-done.2
  108.6 0.0 copy-done.4
  108.7 0.0 copy-start.1
  108.7 3.0 fusion.1
  111.7 0.0 copy-done.1
  111.7 5.2 %convolution_add_fusion = f32[576,3072]{0,1:T(8,128)} fusion(f32[576,3072]{0,1:T(8,128)S(1)} %fusion.1, bf16[1,3072,512]{2,1,0:T(8,128)(2,1)S(1)} %copy-done.1, f32[576,512]{1,0:T(8,128)S(1)} %fusion.3, bf16[1,576,512]{2,1,0:T(8,128)(2,1)S(1)} %copy-done.2), kind=kOutput, calls=%fused_computation | convolution fusion | flops 1816952832 | bytes 19070976 | tf_op jit(solution)/shard_map/dot_general | solution.py:75
  116.9 0.0 copy-start.3
  116.9 0.0 reduce-scatter.2.cloned.1.call-update
  116.9 0.1 reduce_sum.21
  117.1 0.1 copy.36
  117.1 0.4 copy-done.3
  117.6 224.0 %reduce-scatter.2.cloned.1.call-done = f32[576,96]{0,1:T(8,128)} async-done(((f32[576,3072]{0,1:T(8,128)}), f32[576,96]{0,1:T(8,128)}) %reduce-scatter.2.cloned.1.call-update) | async-done | bytes 221200 | tf_op jit(solution)/shard_map/reduce_scatter | solution.py:78
  341.6 1.0 convert_element_type.61
  342.6 0.8 copy.40
  343.3 8.6 %all-to-all-start.1 = ((bf16[8,72,96]{2,1,0:T(8,128)(2,1)}), bf16[8,72,96]{2,1,0:T(8,128)(2,1)S(1)}, u32[]{:S(2)}, u32[]{:S(2)}) async-start(bf16[8,72,96]{2,1,0:T(8,128)(2,1)} %bitcast.11), calls=%async_computation.2 | async-start | bytes 294912 | tf_op jit(solution)/shard_map/all_to_all | solution.py:80
  351.9 0.2 convert_reduce_fusion
  352.1 5.3 %all-to-all-done.1 = bf16[8,72,96]{2,1,0:T(8,128)(2,1)S(1)} async-done(((bf16[8,72,96]{2,1,0:T(8,128)(2,1)}), bf16[8,72,96]{2,1,0:T(8,128)(2,1)S(1)}, u32[]{:S(2)}, u32[]{:S(2)}) %all-to-all-start.1) | async-done | bytes 110624 | tf_op jit(solution)/shard_map/all_to_all | solution.py:80
  357.4 0.8 convolution_convert_fusion.1
  (4 shorter events, 0.1 us)
Async XLA Ops:
  6.5 102.1 %copy-start = (bf16[1,3072,512]{2,1,0:T(8,128)(2,1)S(1)}, bf16[1,3072,512]{2,1,0:T(8,128)(2,1)}, u32[]{:S(2)}) copy-start(bf16[1,3072,512]{2,1,0:T(8,128)(2,1)} %param.13) | copy-start | bytes 9437188
  6.5 96.5 %all-gather.2.cloned.1.call-start = ((), (), s32[]{:S(2)}) async-start(), calls=%async_computation.3 | async-start | bytes 4055040 | tf_op jit(solution)/shard_map/all_gather | solution.py:65
  23.3 318.3 %reduce-scatter.2.cloned.1.call-start = ((), (), s32[]{:S(2)}) async-start(), calls=%async_computation.4 | async-start | bytes 8110080 | tf_op jit(solution)/shard_map/reduce_scatter | solution.py:78
  103.1 5.6 %copy-start.2 = (bf16[1,576,512]{2,1,0:T(8,128)(2,1)S(1)}, bf16[1,576,512]{2,1,0:T(8,128)(2,1)}, u32[]{:S(2)}) copy-start(bf16[1,576,512]{2,1,0:T(8,128)(2,1)} %param.11) | copy-start | bytes 1769476
  103.1 5.6 %copy-start.4 = (bf16[1,576,512]{2,1,0:T(8,128)(2,1)S(1)}, bf16[1,576,512]{2,1,0:T(8,128)(2,1)}, u32[]{:S(2)}) copy-start(bf16[1,576,512]{2,1,0:T(8,128)(2,1)} %param.12) | copy-start | bytes 1769476
  108.7 3.1 copy-start.1
  116.9 0.7 copy-start.3
  343.3 14.0 %all-to-all-start.1 = ((bf16[8,72,96]{2,1,0:T(8,128)(2,1)}), bf16[8,72,96]{2,1,0:T(8,128)(2,1)S(1)}, u32[]{:S(2)}, u32[]{:S(2)}) async-start(bf16[8,72,96]{2,1,0:T(8,128)(2,1)} %bitcast.11), calls=%async_computation.2 | async-start | bytes 294912 | tf_op jit(solution)/shard_map/all_to_all | solution.py:80
Sparse Core Ops, SparseCore 0:
  23.4 79.5 all-gather.1
  117.0 224.5 reduce-scatter.1
where the time goes:
time: 365 us
  waiting for transfers between devices  309 us (85%)
  matrix products  14.9 us (4%)
  between operations  13.5 us (4%)
  blocking collectives  11.2 us (3%)
  starting transfers between devices  8.63 us (2%)
  local copies, waits for them, and re-layouts  5.59 us (2%)
    reduce_scatter x1, waiting for transfers between devices, per_device(): lax.psum_scatter(gate_term + up_term, ('row', 'col'), scatter_dimension=1...  224 us
    all_gather x1, waiting for transfers between devices, per_device(): lax.all_gather(routed, ('row', 'col'), axis=1, tiled=True)  79.7 us
    all_to_all x1, blocking collectives, per_device(): lax.all_to_all(outgoing, 'expert', split_axis=0, concat_axis=0, tiled=True)  11.2 us
    all_to_all x1, starting transfers between devices, per_device(): lax.all_to_all(slot_grad.reshape(experts, capacity, feat_local), 'expert'...  8.59 us
  transfers between devices with their start and end apart: 3, of which 3 were waited for; matrix products, arithmetic and copies ran while one was open for 0% of the time, Pallas kernels for 0%

commit v1 on v0

v1 whole, which is shorter than its diff:
```python
import functools

import jax
import jax.numpy as jnp
from jax import lax
from jax.experimental import pallas as pl
from jax.experimental.pallas import tpu as pltpu
from jax.sharding import PartitionSpec as P

tanh_scale = 0.7978845608028654
cubic_term = 0.044715

MESH = pl.DeviceIdType.MESH
F32 = jnp.float32
BF16 = jnp.bfloat16

NE, NZ, NX = 8, 8, 4
CAP = 72
FD = 96
SLAB = NX * FD
HID = 512
CA, CB, CT = 256, 256, 128
NC = CA + CB + CT
HALF = SLAB // 2


def gelu_pair(pre_act):
    inner_arg = tanh_scale * (pre_act + cubic_term * pre_act * pre_act * pre_act)
    tanh_part = jnp.tanh(inner_arg)
    activation = 0.5 * pre_act * (1.0 + tanh_part)
    derivative = 0.5 * (1.0 + tanh_part) + 0.5 * pre_act * (
        1.0 - tanh_part * tanh_part
    ) * tanh_scale * (1.0 + 3.0 * cubic_term * pre_act * pre_act)
    return (activation, derivative)


def mm(a, b):
    return jnp.dot(a, b, preferred_element_type=F32)


def mm_nt(a, b):
    return lax.dot_general(a, b, (((1,), (1,)), ((), ())), preferred_element_type=F32)


def iota(shape, dim):
    return lax.broadcasted_iota(jnp.int32, shape, dim)


def kernel(
    tok_ref, ids_ref, wts_ref, gs_hbm, us_hbm, gw_hbm, uw_hbm, dw_hbm, out_ref,
    gs, us, gw, uw, dw, act_t, dup_t,
    onehot, place, snd1, rcv1, snd2, rcv2,
    xa, xb, xt, xtu, h, gg, ug, slot_t,
    part, sa, sb, st, ra_p, ra_m, rax, sax, rbx, rtx, qb, qt, rbz_p, rbz_m, rtz_p, rtz_m,
    ld, a1s, a1r, a2s, a2r,
    axs, axr, azps, azpr, azms, azmr,
    bzps, bzpr, bzms, bzmr, bxs, bxr,
    rzps, rzpr, rzms, rzmr, rxs, rxr,
    qzps, qzpr, qzms, qzmr, qxs, qxr,
):
    e = lax.axis_index("expert")
    z = lax.axis_index("row")
    x = lax.axis_index("col")

    def dev(de=0, dz=0, dx=0):
        return (
            lax.rem(e + (de + NE), NE),
            lax.rem(z + (dz + NZ), NZ),
            lax.rem(x + (dx + NX), NX),
        )

    def zrel(d):
        return lax.rem(z + (d + NZ), NZ)

    def xrel(d):
        return lax.rem(x + (d + NX), NX)

    def xrows(xx, size):
        return pl.ds(pl.multiple_of(xx * size, size), size)

    started = []

    def send(src, dst, ss, rs, to):
        copy = pltpu.make_async_remote_copy(
            src_ref=src, dst_ref=dst, send_sem=ss, recv_sem=rs, device_id=to, device_id_type=MESH
        )
        copy.start()
        started.append(copy)
        return copy

    loads = [
        pltpu.make_async_copy(gs_hbm.at[0], gs.at[pl.ds(0, 576)], ld.at[0]),
        pltpu.make_async_copy(us_hbm.at[0], us.at[pl.ds(0, 576)], ld.at[1]),
        pltpu.make_async_copy(dw_hbm.at[0], dw, ld.at[2]),
        pltpu.make_async_copy(gw_hbm.at[0], gw, ld.at[3]),
        pltpu.make_async_copy(uw_hbm.at[0], uw, ld.at[4]),
    ]
    for c in loads:
        c.start()
    bar = pltpu.get_barrier_semaphore()
    partners = [dev(de=r) for r in range(1, NE)]
    partners += [dev(dz=1), dev(dz=-1)] + [dev(dx=r) for r in range(1, NX)]
    for p in partners:
        pl.semaphore_signal(bar, inc=1, device_id=p, device_id_type=MESH)

    tok_t = tok_ref[...].astype(F32).T
    ids = ids_ref[...]
    wts = wts_ref[...]
    e_iota = iota((NE, 192), 0)
    first = ids[0:1, :] == e_iota
    second = ids[1:2, :] == e_iota
    named = jnp.where(first, 1.0, jnp.where(second, 1.0, 0.0))
    weight = jnp.where(first, wts[0:1, :], jnp.where(second, wts[1:2, :], 0.0))
    earlier = jnp.where(iota((192, 192), 0) < iota((192, 192), 1), 1.0, 0.0).astype(BF16)
    pos = mm(named.astype(BF16), earlier)
    pos = jnp.where(named > 0.5, pos, -1.0)
    j_iota = iota((128, 192), 0).astype(F32)
    for i in range(NE):
        oh = jnp.where(pos[i : i + 1, :] == j_iota, 1.0, 0.0).astype(BF16)
        onehot[128 * i : 128 * i + 128, :] = oh
        scaled = (tok_t * weight[i : i + 1, :]).astype(BF16)
        snd1[i] = mm_nt(scaled, oh).astype(BF16)

    pl.semaphore_wait(bar, len(partners))

    a2a = {}
    for r in range(1, NE):
        to = lax.rem(e + r, NE)
        a2a[r] = send(snd1.at[to], rcv1.at[e], a1s.at[r], a1r.at[r], dev(de=r))
    rcv1[e] = snd1[e]
    pj = iota((128, NC), 0)
    pc = iota((128, NC), 1)
    for s in range(NE):
        place[128 * s : 128 * s + 128, :] = jnp.where(
            (pc == pj + CAP * s) & (pj < CAP), 1.0, 0.0
        ).astype(BF16)
    gs[576:640, :] = jnp.zeros((64, HID), BF16)
    us[576:640, :] = jnp.zeros((64, HID), BF16)
    h[...] = jnp.zeros_like(h)
    for r in range(1, NE):
        a2a[r].wait_recv()
    rows = mm(rcv1[0], place[0:128, :])
    for s in range(1, NE):
        rows += mm(rcv1[s], place[128 * s : 128 * s + 128, :])
    xa[z, xrows(x, FD), :] = rows[:, :CA].astype(BF16)
    xb[z, xrows(x, FD), :] = rows[:, CA : CA + CB].astype(BF16)
    tail = rows[:, CA + CB :]
    xt[z, xrows(x, FD // 2), :] = (tail[: FD // 2] + pltpu.roll(tail[FD // 2 :], 64, 1)).astype(BF16)

    def gelu_block(b):
        def body(c, carry):
            cols = pl.ds(pl.multiple_of(c * 128, 128), 128)
            act, der = gelu_pair(gs[128 * b : 128 * b + 128, cols].astype(F32))
            der = der * us[128 * b : 128 * b + 128, cols].astype(F32)
            act_t[cols, 128 * b : 128 * b + 128] = act.T
            dup_t[cols, 128 * b : 128 * b + 128] = der.T
            return carry

        lax.fori_loop(0, HID // 128, body, 0)

    def both(k, body):
        if k in (0, 4):
            body(zrel(k))
        else:
            def step(i, carry):
                body(lax.rem(z + NZ + k - 2 * k * i, NZ))
                return carry

            lax.fori_loop(0, 2, step, 0)

    def mm_a(zz):
        cols = pl.ds(pl.multiple_of(zz * SLAB, SLAB), SLAB)
        h[:, :CA] += mm(dw[:, cols], xa[zz])

    def mm_b(zz):
        cols = pl.ds(pl.multiple_of(zz * SLAB, SLAB), SLAB)
        low = iota((FD // 2, 128), 1) < 64
        for i in range(NX):
            t = xt[zz, i * (FD // 2) : (i + 1) * (FD // 2), :].astype(F32)
            xtu[zz, FD * i : FD * i + FD // 2, :] = jnp.where(low, t, 0.0).astype(BF16)
            xtu[zz, FD * i + FD // 2 : FD * i + FD, :] = jnp.where(
                low, pltpu.roll(t, 64, 1), 0.0
            ).astype(BF16)
        h[:, CA : CA + CB] += mm(dw[:, cols], xb[zz])
        h[:, CA + CB :] += mm(dw[:, cols], xtu[zz])

    def bz(zz, to_plus, k):
        ss, rs, to = (bzps, bzpr, dev(dz=1)) if to_plus else (bzms, bzmr, dev(dz=-1))
        m = xb.at[zz, xrows(x, FD)]
        t = xt.at[zz, xrows(x, FD // 2)]
        return (send(m, m, ss.at[0, k], rs.at[0, k], to), send(t, t, ss.at[1, k], rs.at[1, k], to))

    def bx(d, xx, which, dx):
        i = d % NZ
        m = xb.at[zrel(d), xrows(xx, FD)]
        t = xt.at[zrel(d), xrows(xx, FD // 2)]
        to = dev(dx=dx)
        return (
            send(m, m, bxs.at[i, which, 0], bxr.at[i, which, 0], to),
            send(t, t, bxs.at[i, which, 1], bxr.at[i, which, 1], to),
        )

    def got(pair):
        for c in pair:
            c.wait_recv()

    bzp, bzm, bxc, azp, azm = {}, {}, {}, {}, {}
    bzp[0] = bz(z, True, 0)
    bzm[0] = bz(z, False, 0)
    own = xa.at[z, xrows(x, FD)]
    ax = [send(own, own, axs.at[r], axr.at[r], dev(dx=r)) for r in range(1, NX)]

    def bx_first(d):
        bxc[d, 0] = bx(d, x, 0, 1)
        bxc[d, 1] = bx(d, x, 1, -1)

    def bx_second(d):
        if d % 2 == 0:
            got(bxc[d, 0])
            bxc[d, 2] = bx(d, xrel(-1), 2, 1)
        else:
            got(bxc[d, 1])
            bxc[d, 2] = bx(d, xrel(1), 2, -1)

    def bx_done(d):
        got(bxc[d, 1 if d % 2 == 0 else 0])
        got(bxc[d, 2])

    def az(zz, to_plus, k, part_rows=None):
        ss, rs, to = (azps, azpr, dev(dz=1)) if to_plus else (azms, azmr, dev(dz=-1))
        m = xa.at[zz] if part_rows is None else xa.at[zz, part_rows]
        return send(m, m, ss.at[k], rs.at[k], to)

    def ds(k):
        return (k,) if k in (0, 4) else (-k, k)

    bx_first(0)
    for c in loads[:2]:
        c.wait()
    for c in ax:
        c.wait_recv()
    azp[0] = az(z, True, 0)
    azm[0] = az(z, False, 0)
    gelu_block(0)
    loads[2].wait()

    for k in range(1, 5):
        got(bzp[k - 1])
        if k <= 3:
            bzp[k] = bz(zrel(-k), True, k)
            got(bzm[k - 1])
            if k <= 2:
                bzm[k] = bz(zrel(k), False, k)
        for d in ds(k):
            bx_first(d)
        for d in ds(k - 1):
            bx_second(d)
        both(k - 1, mm_a)
        if k >= 2:
            for d in ds(k - 2):
                bx_done(d)
            both(k - 2, mm_b)
        gelu_block(k)
        azp[k - 1].wait_recv()
        if k <= 3:
            azp[k] = az(zrel(-k), True, k, None if k <= 2 else pl.ds(0, HALF))
        azm[k - 1].wait_recv()
        if k <= 3:
            azm[k] = az(zrel(k), False, k, None if k <= 2 else pl.ds(HALF, HALF))
    for d in ds(4):
        bx_second(d)
    both(4, mm_a)
    for d in ds(3):
        bx_done(d)
    both(3, mm_b)
    for d in ds(4):
        bx_done(d)
    both(4, mm_b)

    gg[...] = (h[...] * dup_t[...]).astype(BF16)
    ug[...] = (h[...] * act_t[...]).astype(BF16)
    for c in loads[3:]:
        c.wait()

    def mm_p(zz):
        r = pl.ds(pl.multiple_of(zz * SLAB, SLAB), SLAB)
        p = mm(gw[r, :], gg[...]) + mm(uw[r, :], ug[...])
        part[zz] = p
        sb[zz] = p[:, CA : CA + CB].astype(BF16)
        t = p[:, CA + CB :]
        for i in range(NX):
            st[zz, i * (FD // 2) : (i + 1) * (FD // 2), :] = (
                t[FD * i : FD * i + FD // 2] + pltpu.roll(t[FD * i + FD // 2 : FD * i + FD], 64, 1)
            ).astype(BF16)

    def ra(k, to_plus, rows_):
        zz = zrel(4 - k) if to_plus else zrel(k - 4)
        ss, rs, to, rb = (
            (rzps, rzpr, dev(dz=1), ra_p) if to_plus else (rzms, rzmr, dev(dz=-1), ra_m)
        )
        return send(sa.at[zz, rows_], rb.at[k, rows_], ss.at[k], rs.at[k], to)

    def rx(d, xx, which, dx):
        i = d % NZ
        zz = zrel(d)
        to = dev(dx=dx)
        return (
            send(sb.at[zz, xrows(xx, FD)], rbx.at[i, which], rxs.at[i, which, 0], rxr.at[i, which, 0], to),
            send(st.at[zz, xrows(xx, FD // 2)], rtx.at[i, which], rxs.at[i, which, 1], rxr.at[i, which, 1], to),
        )

    rxc = {}

    def rx_first(d):
        s = 1 if d % 2 == 0 else -1
        rxc[d, 0] = rx(d, xrel(2), 0, s)
        rxc[d, 1] = rx(d, xrel(-s), 1, -s)

    def tail_of(zz, xx):
        base = pl.multiple_of(xx * FD, FD // 2)
        top = part[zz, pl.ds(base, FD // 2), CA + CB :]
        bot = part[zz, pl.ds(pl.multiple_of(base + FD // 2, FD // 2), FD // 2), CA + CB :]
        return top + pltpu.roll(bot, 64, 1)

    def rx_second(d):
        s = 1 if d % 2 == 0 else -1
        i = d % NZ
        zz = zrel(d)
        xx = xrel(s)
        got(rxc[d, 0])
        sb[zz, xrows(xx, FD), :] = (
            part[zz, xrows(xx, FD), CA : CA + CB] + rbx[i, 0].astype(F32)
        ).astype(BF16)
        st[zz, xrows(xx, FD // 2), :] = (tail_of(zz, xx) + rtx[i, 0].astype(F32)).astype(BF16)
        rxc[d, 2] = rx(d, xx, 2, s)

    def rx_done(d):
        i = d % NZ
        zz = zrel(d)
        got(rxc[d, 1])
        got(rxc[d, 2])
        m = part[zz, xrows(x, FD), CA : CA + CB] + rbx[i, 1].astype(F32) + rbx[i, 2].astype(F32)
        t = tail_of(zz, x) + rtx[i, 1].astype(F32) + rtx[i, 2].astype(F32)
        return m, t

    qc = {}

    def q_send(k, to_plus, m, t):
        i = (4 - k) % NZ if to_plus else (k - 4) % NZ
        qb[i] = m.astype(BF16)
        qt[i] = t.astype(BF16)
        ss, rs, to, rb, rt = (
            (qzps, qzpr, dev(dz=1), rbz_p, rtz_p)
            if to_plus
            else (qzms, qzmr, dev(dz=-1), rbz_m, rtz_m)
        )
        qc[k, to_plus] = (
            send(qb.at[i], rb.at[k], ss.at[0, k], rs.at[0, k], to),
            send(qt.at[i], rt.at[k], ss.at[1, k], rs.at[1, k], to),
        )

    def q_stage(k):
        if k == 0:
            m, t = rx_done(4)
            q_send(0, True, m, t)
            return
        m, t = rx_done(4 - k)
        got(qc[k - 1, True])
        q_send(k, True, m + rbz_p[k - 1].astype(F32), t + rtz_p[k - 1].astype(F32))
        m, t = rx_done(k - 4)
        if k >= 2:
            got(qc[k - 1, False])
            m = m + rbz_m[k - 1].astype(F32)
            t = t + rtz_m[k - 1].astype(F32)
        q_send(k, False, m, t)

    rap, ram = {}, {}
    lo, hi, full = pl.ds(0, HALF), pl.ds(HALF, HALF), pl.ds(0, SLAB)
    for k in range(4):
        both(4 - k, mm_p)
        if k == 0:
            sa[zrel(4)] = part[zrel(4), :, :CA].astype(BF16)
            rap[0] = ra(0, True, lo)
            ram[0] = ra(0, False, hi)
        else:
            zp, zm = zrel(4 - k), zrel(k - 4)
            rap[k - 1].wait_recv()
            if k == 1:
                sa[zp, :HALF] = (part[zp, :HALF, :CA] + ra_p[0, :HALF].astype(F32)).astype(BF16)
                sa[zp, HALF:] = part[zp, HALF:, :CA].astype(BF16)
            else:
                sa[zp] = (part[zp, :, :CA] + ra_p[k - 1].astype(F32)).astype(BF16)
            rap[k] = ra(k, True, full)
            ram[k - 1].wait_recv()
            if k == 1:
                sa[zm, :HALF] = part[zm, :HALF, :CA].astype(BF16)
                sa[zm, HALF:] = (part[zm, HALF:, :CA] + ra_m[0, HALF:].astype(F32)).astype(BF16)
            else:
                sa[zm] = (part[zm, :, :CA] + ra_m[k - 1].astype(F32)).astype(BF16)
            ram[k] = ra(k, False, full)
        for d in ds(4 - k):
            rx_first(d)
        if k >= 1:
            for d in ds(5 - k):
                rx_second(d)
        if k >= 2:
            q_stage(k - 2)
    both(0, mm_p)
    rx_first(0)
    for d in ds(1):
        rx_second(d)
    q_stage(2)
    rap[3].wait_recv()
    ram[3].wait_recv()
    part[z, :, :CA] = part[z, :, :CA] + ra_p[3].astype(F32) + ra_m[3].astype(F32)
    sax[...] = part[z, :, :CA].astype(BF16)
    sx = [
        send(sax.at[xrows(xrel(r), FD)], rax.at[r], qxs.at[r], qxr.at[r], dev(dx=r))
        for r in range(1, NX)
    ]
    rx_second(0)
    q_stage(3)
    m, t = rx_done(0)
    for c in sx:
        c.wait_recv()
    a = part[z, xrows(x, FD), :CA]
    for r in range(1, NX):
        a = a + rax[r].astype(F32)
    slot_t[:, :CA] = a.astype(BF16)
    got(qc[3, True])
    got(qc[3, False])
    m = m + rbz_p[3].astype(F32) + rbz_m[3].astype(F32)
    t = t + rtz_p[3].astype(F32) + rtz_m[3].astype(F32)
    slot_t[:, CA : CA + CB] = m.astype(BF16)
    low = iota((FD // 2, 128), 1) < 64
    slot_t[: FD // 2, CA + CB :] = jnp.where(low, t, 0.0).astype(BF16)
    slot_t[FD // 2 :, CA + CB :] = jnp.where(low, pltpu.roll(t, 64, 1), 0.0).astype(BF16)

    for s in range(NE):
        snd2[s] = mm_nt(slot_t[...], place[128 * s : 128 * s + 128, :]).astype(BF16)
    back = {}
    for r in range(1, NE):
        to = lax.rem(e + r, NE)
        back[r] = send(snd2.at[to], rcv2.at[e], a2s.at[r], a2r.at[r], dev(de=r))
    rcv2[e] = snd2[e]
    for r in range(1, NE):
        back[r].wait_recv()
    o = mm(rcv2[0], onehot[0:128, :])
    for s in range(1, NE):
        o += mm(rcv2[s], onehot[128 * s : 128 * s + 128, :])
    out_ref[...] = o.T.astype(BF16)
    for c in started:
        c.wait_send()


def per_device(tokens_grad, expert_ids, combine_weights, gate_saved, up_saved, gate_weight, up_weight, down_weight):
    vmem = pl.BlockSpec(memory_space=pltpu.VMEM)
    hbm = pl.BlockSpec(memory_space=pl.ANY)
    dma = pltpu.SemaphoreType.DMA
    v = pltpu.VMEM
    scratch = [
        v((640, HID), BF16), v((640, HID), BF16),
        v((3072, HID), BF16), v((3072, HID), BF16), v((HID, 3072), BF16),
        v((HID, NC), F32), v((HID, NC), F32),
        v((1024, 192), BF16), v((1024, NC), BF16),
        v((NE, FD, 128), BF16), v((NE, FD, 128), BF16), v((NE, FD, 128), BF16), v((NE, FD, 128), BF16),
        v((NZ, SLAB, CA), BF16), v((NZ, SLAB, CB), BF16), v((NZ, HALF, CT), BF16), v((NZ, SLAB, CT), BF16),
        v((HID, NC), F32), v((HID, NC), BF16), v((HID, NC), BF16), v((FD, NC), BF16),
        v((NZ, SLAB, NC), F32),
        v((NZ, SLAB, CA), BF16), v((NZ, SLAB, CB), BF16), v((NZ, HALF, CT), BF16),
        v((4, SLAB, CA), BF16), v((4, SLAB, CA), BF16),
        v((NX, FD, CA), BF16), v((SLAB, CA), BF16),
        v((NZ, 3, FD, CB), BF16), v((NZ, 3, FD // 2, CT), BF16),
        v((NZ, FD, CB), BF16), v((NZ, FD // 2, CT), BF16),
        v((4, FD, CB), BF16), v((4, FD, CB), BF16), v((4, FD // 2, CT), BF16), v((4, FD // 2, CT), BF16),
        dma((5,)),
        dma((NE,)), dma((NE,)), dma((NE,)), dma((NE,)),
        dma((NX,)), dma((NX,)), dma((4,)), dma((4,)), dma((4,)), dma((4,)),
        dma((2, 4)), dma((2, 4)), dma((2, 4)), dma((2, 4)), dma((NZ, 3, 2)), dma((NZ, 3, 2)),
        dma((4,)), dma((4,)), dma((4,)), dma((4,)), dma((NZ, 3, 2)), dma((NZ, 3, 2)),
        dma((2, 4)), dma((2, 4)), dma((2, 4)), dma((2, 4)), dma((NX,)), dma((NX,)),
    ]
    return pl.pallas_call(
        kernel,
        out_shape=jax.ShapeDtypeStruct(tokens_grad.shape, BF16),
        in_specs=[vmem] * 3 + [hbm] * 5,
        out_specs=vmem,
        scratch_shapes=scratch,
        compiler_params=pltpu.CompilerParams(
            collective_id=0, has_side_effects=True, vmem_limit_bytes=60 * 2**20
        ),
        name="moe_backward",
    )(tokens_grad, expert_ids.T, combine_weights.T, gate_saved, up_saved, gate_weight, up_weight, down_weight)


def solution(mesh):
    in_specs = (
        P("expert", ("row", "col")),
        P("expert", None),
        P("expert", None),
        P("expert", None, ("row", "col")),
        P("expert", None, ("row", "col")),
        P("expert", None, ("row", "col")),
        P("expert", None, ("row", "col")),
        P("expert", ("row", "col"), None),
    )
    out_specs = P("expert", ("row", "col"))
    return jax.shard_map(
        per_device, mesh=mesh, in_specs=in_specs, out_specs=out_specs, check_vma=False
    )
```

time: 365 us -> 88.9 us (0.24)
  waiting for transfers between devices: 309 us -> 0 us
  Pallas kernels: 0 us -> 87.3 us
  matrix products: 14.9 us -> 0 us
  between operations: 13.5 us -> 0.01 us
  blocking collectives: 11.2 us -> 0 us
  starting transfers between devices: 8.63 us -> 0 us
  local copies, waits for them, and re-layouts: 5.59 us -> 1.42 us
    reduce_scatter x1 -> x0, waiting for transfers between devices: 224 us -> none  [per_device(): lax.psum_scatter(gate_term + up_term, ('row', 'col'), scatter_dimension=1...]
    pallas_call x0 -> x1, Pallas kernels: none -> 87.3 us  [per_device(): pl.pallas_call(kernel, out_shape=jax.ShapeDtypeStruct(tokens_grad.shape,...]
    all_gather x1 -> x0, waiting for transfers between devices: 79.7 us -> none  [per_device(): lax.all_gather(routed, ('row', 'col'), axis=1, tiled=True)]
    dot_general x5 -> x0, matrix products: 14.9 us -> none  [the longest x1 5.56 us: per_device(): lax.dot_general(lax.all_gather(routed, ('row', 'col'), axis=1, tiled=True...]
    all_to_all x1 -> x0, blocking collectives: 11.2 us -> none  [per_device(): lax.all_to_all(outgoing, 'expert', split_axis=0, concat_axis=0, tiled=True)]
    all_to_all x1 -> x0, starting transfers between devices: 8.59 us -> none  [per_device(): lax.all_to_all(slot_grad.reshape(experts, capacity, feat_local), 'expert'...]
    all_to_all x1 -> x0, waiting for transfers between devices: 5.26 us -> none  [per_device(): lax.all_to_all(slot_grad.reshape(experts, capacity, feat_local), 'expert'...]
  transfers between devices with their start and end apart: 3 -> 0, of which waited for: 3 -> 0; matrix products, arithmetic and copies ran while one was open for 0% -> 0% of each run, Pallas kernels for 0% -> 0%
where the time goes in v1:
time: 88.9 us; the launch traced here: 88.7 us
  Pallas kernels  87.3 us (98%)
  local copies, waits for them, and re-layouts  1.42 us (2%)
    pallas_call x1, Pallas kernels, per_device(): pl.pallas_call(kernel, out_shape=jax.ShapeDtypeStruct(tokens_grad.shape,...  87.3 us

profile of v1, /device:TPU:1, one launch (start us, length us, event | category | flops | bytes accessed | tf_op | source)
XLA Modules:
  0.0 88.7 jit_solution(10812976074243706586)
XLA Ops:
  0.0 87.3 %moe_backward.1 = bf16[192,96]{1,0:T(8,128)(2,1)} custom-call(bf16[192,96]{1,0:T(8,128)(2,1)} %tok_ref.1, s32[2,192]{1,0:T(2,128)} %bitcast.2, f32[2,192]{1,0:T(2,128)} %bitcast.3, bf16[1,576,512]{2,1,0:T(8,128)(2,1)} %gs_hbm.1, bf16[1,576,512]{2,1,0:T(8,128)(2,1)} %us_hbm.1, bf16[1,3072,512]{2,1,0:T(8,128)(2,1)} %gw_hbm.1, bf16[1,3072,512]{2,1,0:T(8,128)(2,1)} %uw_hbm.1, ...), custom_call_target="tpu_custom_call" | custom-call | tf_op jit(solution)/shard_map/moe_backward/pallas_call | solution.py:483
  87.3 1.4 %copy.10 = bf16[192,96]{1,0:T(8,128)(2,1)} copy(bf16[192,96]{1,0:T(8,128)(2,1)} %moe_backward.1) | data formatting | bytes 73728

commit v2 on v1

--- a/solution.py
+++ b/solution.py
@@ -47,8 +47,8 @@
 
 
 def kernel(
-    tok_ref, ids_ref, wts_ref, gs_hbm, us_hbm, gw_hbm, uw_hbm, dw_hbm, out_ref,
-    gs, us, gw, uw, dw, act_t, dup_t,
+    tok_hbm, ids_hbm, wts_hbm, gs_hbm, us_hbm, gw_hbm, uw_hbm, dw_hbm, out_ref,
+    tok_ref, ids_ref, wts_ref, gs, us, gw, uw, dw, act_t, dup_t,
     onehot, place, snd1, rcv1, snd2, rcv2,
     xa, xb, xt, xtu, h, gg, ug, slot_t,
     part, sa, sb, st, ra_p, ra_m, rax, sax, rbx, rtx, qb, qt, rbz_p, rbz_m, rtz_p, rtz_m,
@@ -88,6 +88,16 @@
         started.append(copy)
         return copy
 
+    bar = pltpu.get_barrier_semaphore()
+    partners = [dev(dz=1), dev(dz=-1)] + [dev(dx=r) for r in range(1, NX)]
+    partners += [dev(de=r) for r in range(1, NE)]
+    for p in partners:
+        pl.semaphore_signal(bar, inc=1, device_id=p, device_id_type=MESH)
+    small = [
+        pltpu.make_async_copy(tok_hbm, tok_ref, ld.at[5]),
+        pltpu.make_async_copy(ids_hbm, ids_ref, ld.at[6]),
+        pltpu.make_async_copy(wts_hbm, wts_ref, ld.at[7]),
+    ]
     loads = [
         pltpu.make_async_copy(gs_hbm.at[0], gs.at[pl.ds(0, 576)], ld.at[0]),
         pltpu.make_async_copy(us_hbm.at[0], us.at[pl.ds(0, 576)], ld.at[1]),
@@ -95,13 +105,10 @@
         pltpu.make_async_copy(gw_hbm.at[0], gw, ld.at[3]),
         pltpu.make_async_copy(uw_hbm.at[0], uw, ld.at[4]),
     ]
-    for c in loads:
+    for c in small + loads:
         c.start()
-    bar = pltpu.get_barrier_semaphore()
-    partners = [dev(de=r) for r in range(1, NE)]
-    partners += [dev(dz=1), dev(dz=-1)] + [dev(dx=r) for r in range(1, NX)]
-    for p in partners:
-        pl.semaphore_signal(bar, inc=1, device_id=p, device_id_type=MESH)
+    for c in small:
+        c.wait()
 
     tok_t = tok_ref[...].astype(F32).T
     ids = ids_ref[...]
@@ -205,10 +212,6 @@
             c.wait_recv()
 
     bzp, bzm, bxc, azp, azm = {}, {}, {}, {}, {}
-    bzp[0] = bz(z, True, 0)
-    bzm[0] = bz(z, False, 0)
-    own = xa.at[z, xrows(x, FD)]
-    ax = [send(own, own, axs.at[r], axr.at[r], dev(dx=r)) for r in range(1, NX)]
 
     def bx_first(d):
         bxc[d, 0] = bx(d, x, 0, 1)
@@ -226,25 +229,28 @@
         got(bxc[d, 1 if d % 2 == 0 else 0])
         got(bxc[d, 2])
 
-    def az(zz, to_plus, k, part_rows=None):
+    def az(zz, j, to_plus, k):
         ss, rs, to = (azps, azpr, dev(dz=1)) if to_plus else (azms, azmr, dev(dz=-1))
-        m = xa.at[zz] if part_rows is None else xa.at[zz, part_rows]
-        return send(m, m, ss.at[k], rs.at[k], to)
+        m = xa.at[zz, xrows(xrel(j), FD)]
+        return send(m, m, ss.at[k, j], rs.at[k, j], to)
 
     def ds(k):
         return (k,) if k in (0, 4) else (-k, k)
 
+    order = (0, 1, 3, 2)
+    plus_last, minus_last = order[:2], order[2:]
+
+    bzp[0] = bz(z, True, 0)
+    bzm[0] = bz(z, False, 0)
+    azp[0, 0] = az(z, 0, True, 0)
+    azm[0, 0] = az(z, 0, False, 0)
+    own = xa.at[z, xrows(x, FD)]
+    ax = {r: send(own, own, axs.at[r], axr.at[r], dev(dx=r)) for r in (1, 3, 2)}
     bx_first(0)
     for c in loads[:2]:
         c.wait()
-    for c in ax:
-        c.wait_recv()
-    azp[0] = az(z, True, 0)
-    azm[0] = az(z, False, 0)
-    gelu_block(0)
-    loads[2].wait()
-
-    for k in range(1, 5):
+
+    def b_step(k):
         got(bzp[k - 1])
         if k <= 3:
             bzp[k] = bz(zrel(-k), True, k)
@@ -253,52 +259,108 @@
                 bzm[k] = bz(zrel(k), False, k)
         for d in ds(k):
             bx_first(d)
-        for d in ds(k - 1):
+
+    def a_step(k, i):
+        jp, jm = order[i], order[i]
+        if k == 4:
+            jm = order[i + 2]
+        azp[k - 1, jp].wait_recv()
+        if k <= 2 or (k == 3 and jp in plus_last):
+            azp[k, jp] = az(zrel(-k), jp, True, k)
+        azm[k - 1, jm].wait_recv()
+        if k <= 2 or (k == 3 and jm in minus_last):
+            azm[k, jm] = az(zrel(k), jm, False, k)
+
+    def second(k):
+        for d in ds(k):
             bx_second(d)
-        both(k - 1, mm_a)
-        if k >= 2:
-            for d in ds(k - 2):
-                bx_done(d)
-            both(k - 2, mm_b)
-        gelu_block(k)
-        azp[k - 1].wait_recv()
-        if k <= 3:
-            azp[k] = az(zrel(-k), True, k, None if k <= 2 else pl.ds(0, HALF))
-        azm[k - 1].wait_recv()
-        if k <= 3:
-            azm[k] = az(zrel(k), False, k, None if k <= 2 else pl.ds(HALF, HALF))
-    for d in ds(4):
-        bx_second(d)
+
+    def done(k):
+        for d in ds(k):
+            bx_done(d)
+        both(k, mm_b)
+
+    for j in order[1:]:
+        ax[NX - j].wait_recv()
+        azp[0, j] = az(z, j, True, 0)
+        azm[0, j] = az(z, j, False, 0)
+    b_step(1)
+    second(0)
+    gelu_block(0)
+    a_step(1, 0)
+    loads[2].wait()
+    both(0, mm_a)
+    b_step(2)
+    a_step(1, 1)
+    gelu_block(1)
+    a_step(1, 2)
+    second(1)
+    a_step(1, 3)
+    a_step(2, 0)
+    done(0)
+    b_step(3)
+    both(1, mm_a)
+    a_step(2, 1)
+    gelu_block(2)
+    a_step(2, 2)
+    second(2)
+    a_step(2, 3)
+    done(1)
+    b_step(4)
+    a_step(3, 0)
+    both(2, mm_a)
+    a_step(3, 1)
+    gelu_block(3)
+    a_step(3, 2)
+    second(3)
+    a_step(3, 3)
+    done(2)
+    gelu_block(4)
+    both(3, mm_a)
+    a_step(4, 0)
+    second(4)
+    a_step(4, 1)
     both(4, mm_a)
-    for d in ds(3):
-        bx_done(d)
-    both(3, mm_b)
-    for d in ds(4):
-        bx_done(d)
-    both(4, mm_b)
-
-    gg[...] = (h[...] * dup_t[...]).astype(BF16)
-    ug[...] = (h[...] * act_t[...]).astype(BF16)
+
+    def hidden(cols):
+        hh = h[:, cols]
+        gg[:, cols] = (hh * dup_t[:, cols]).astype(BF16)
+        ug[:, cols] = (hh * act_t[:, cols]).astype(BF16)
+
+    hidden(slice(0, CA))
     for c in loads[3:]:
         c.wait()
 
-    def mm_p(zz):
+    def mm_pa(zz):
         r = pl.ds(pl.multiple_of(zz * SLAB, SLAB), SLAB)
-        p = mm(gw[r, :], gg[...]) + mm(uw[r, :], ug[...])
-        part[zz] = p
-        sb[zz] = p[:, CA : CA + CB].astype(BF16)
-        t = p[:, CA + CB :]
+        part[zz, :, :CA] = mm(gw[r, :], gg[:, :CA]) + mm(uw[r, :], ug[:, :CA])
+
+    def mm_pb(zz):
+        r = pl.ds(pl.multiple_of(zz * SLAB, SLAB), SLAB)
+        p = mm(gw[r, :], gg[:, CA : CA + CB]) + mm(uw[r, :], ug[:, CA : CA + CB])
+        part[zz, :, CA : CA + CB] = p
+        sb[zz] = p.astype(BF16)
+        t = mm(gw[r, :], gg[:, CA + CB :]) + mm(uw[r, :], ug[:, CA + CB :])
+        part[zz, :, CA + CB :] = t
         for i in range(NX):
             st[zz, i * (FD // 2) : (i + 1) * (FD // 2), :] = (
                 t[FD * i : FD * i + FD // 2] + pltpu.roll(t[FD * i + FD // 2 : FD * i + FD], 64, 1)
             ).astype(BF16)
 
-    def ra(k, to_plus, rows_):
+    rap, ram = {}, {}
+
+    def ra(k, j, to_plus):
         zz = zrel(4 - k) if to_plus else zrel(k - 4)
-        ss, rs, to, rb = (
-            (rzps, rzpr, dev(dz=1), ra_p) if to_plus else (rzms, rzmr, dev(dz=-1), ra_m)
-        )
-        return send(sa.at[zz, rows_], rb.at[k, rows_], ss.at[k], rs.at[k], to)
+        ss, rs, to, rb, kept = (
+            (rzps, rzpr, dev(dz=1), ra_p, rap) if to_plus else (rzms, rzmr, dev(dz=-1), ra_m, ram)
+        )
+        r = xrows(xrel(j), FD)
+        v = part[zz, r, :CA]
+        if (k - 1, j) in kept:
+            kept[k - 1, j].wait_recv()
+            v = v + rb[k - 1, r].astype(F32)
+        sa[zz, r] = v.astype(BF16)
+        kept[k, j] = send(sa.at[zz, r], rb.at[k, r], ss.at[k, j], rs.at[k, j], to)
 
     def rx(d, xx, which, dx):
         i = d % NZ
@@ -374,59 +436,77 @@
             t = t + rtz_m[k - 1].astype(F32)
         q_send(k, False, m, t)
 
-    rap, ram = {}, {}
-    lo, hi, full = pl.ds(0, HALF), pl.ds(HALF, HALF), pl.ds(0, SLAB)
-    for k in range(4):
-        both(4 - k, mm_p)
-        if k == 0:
-            sa[zrel(4)] = part[zrel(4), :, :CA].astype(BF16)
-            rap[0] = ra(0, True, lo)
-            ram[0] = ra(0, False, hi)
+    orders_p = ((2, 0), (3, 1, 2, 0), (3, 2, 1, 0), (2, 3, 1, 0))
+    orders_m = ((3, 1), (2, 0, 3, 1), (2, 3, 0, 1), (2, 3, 1, 0))
+
+    def ra_both(k, i):
+        ra(k, orders_p[k][i], True)
+        ra(k, orders_m[k][i], False)
+
+    def firsts(k):
+        both(k, mm_pb)
+        for d in ds(k):
+            rx_first(d)
+
+    def seconds(k):
+        for d in ds(k):
+            rx_second(d)
+
+    both(4, mm_pa)
+    ra_both(0, 0)
+    ra_both(0, 1)
+    done(3)
+    both(3, mm_pa)
+    ra_both(1, 0)
+    ra_both(1, 1)
+    done(4)
+    hidden(slice(CA, NC))
+    firsts(4)
+    ra_both(1, 2)
+    ra_both(1, 3)
+    firsts(3)
+    both(2, mm_pa)
+    ra_both(2, 0)
+    seconds(4)
+    ra_both(2, 1)
+    firsts(2)
+    seconds(3)
+    ra_both(2, 2)
+    ra_both(2, 3)
+    q_stage(0)
+    both(1, mm_pa)
+    ra_both(3, 0)
+    firsts(1)
+    seconds(2)
+    ra_both(3, 1)
+    ra_both(3, 2)
+    q_stage(1)
+    firsts(0)
+    ra_both(3, 3)
+    both(0, mm_pa)
+    seconds(1)
+    sx = []
+    own_a = []
+
+    def final_a(j):
+        rap[3, j].wait_recv()
+        ram[3, j].wait_recv()
+        r = xrows(xrel(j), FD)
+        v = part[z, r, :CA] + ra_p[3, r].astype(F32) + ra_m[3, r].astype(F32)
+        if j:
+            sax[r, :] = v.astype(BF16)
+            sx.append(send(sax.at[r], rax.at[j], qxs.at[j], qxr.at[j], dev(dx=j)))
         else:
-            zp, zm = zrel(4 - k), zrel(k - 4)
-            rap[k - 1].wait_recv()
-            if k == 1:
-                sa[zp, :HALF] = (part[zp, :HALF, :CA] + ra_p[0, :HALF].astype(F32)).astype(BF16)
-                sa[zp, HALF:] = part[zp, HALF:, :CA].astype(BF16)
-            else:
-                sa[zp] = (part[zp, :, :CA] + ra_p[k - 1].astype(F32)).astype(BF16)
-            rap[k] = ra(k, True, full)
-            ram[k - 1].wait_recv()
-            if k == 1:
-                sa[zm, :HALF] = part[zm, :HALF, :CA].astype(BF16)
-                sa[zm, HALF:] = (part[zm, HALF:, :CA] + ra_m[0, HALF:].astype(F32)).astype(BF16)
-            else:
-                sa[zm] = (part[zm, :, :CA] + ra_m[k - 1].astype(F32)).astype(BF16)
-            ram[k] = ra(k, False, full)
-        for d in ds(4 - k):
-            rx_first(d)
-        if k >= 1:
-            for d in ds(5 - k):
-                rx_second(d)
-        if k >= 2:
-            q_stage(k - 2)
-    both(0, mm_p)
-    rx_first(0)
-    for d in ds(1):
-        rx_second(d)
+            own_a.append(v)
+
+    final_a(2)
     q_stage(2)
-    rap[3].wait_recv()
-    ram[3].wait_recv()
-    part[z, :, :CA] = part[z, :, :CA] + ra_p[3].astype(F32) + ra_m[3].astype(F32)
-    sax[...] = part[z, :, :CA].astype(BF16)
-    sx = [
-        send(sax.at[xrows(xrel(r), FD)], rax.at[r], qxs.at[r], qxr.at[r], dev(dx=r))
-        for r in range(1, NX)
-    ]
-    rx_second(0)
+    final_a(3)
+    seconds(0)
+    final_a(1)
     q_stage(3)
+    final_a(0)
     m, t = rx_done(0)
-    for c in sx:
-        c.wait_recv()
-    a = part[z, xrows(x, FD), :CA]
-    for r in range(1, NX):
-        a = a + rax[r].astype(F32)
-    slot_t[:, :CA] = a.astype(BF16)
     got(qc[3, True])
     got(qc[3, False])
     m = m + rbz_p[3].astype(F32) + rbz_m[3].astype(F32)
@@ -435,6 +515,12 @@
     low = iota((FD // 2, 128), 1) < 64
     slot_t[: FD // 2, CA + CB :] = jnp.where(low, t, 0.0).astype(BF16)
     slot_t[FD // 2 :, CA + CB :] = jnp.where(low, pltpu.roll(t, 64, 1), 0.0).astype(BF16)
+    a = own_a[0]
+    for c in sx:
+        c.wait_recv()
+    for r in range(1, NX):
+        a = a + rax[r].astype(F32)
+    slot_t[:, :CA] = a.astype(BF16)
 
     for s in range(NE):
         snd2[s] = mm_nt(slot_t[...], place[128 * s : 128 * s + 128, :]).astype(BF16)
@@ -459,6 +545,7 @@
     dma = pltpu.SemaphoreType.DMA
     v = pltpu.VMEM
     scratch = [
+        v((192, FD), BF16), v((2, 192), jnp.int32), v((2, 192), F32),
         v((640, HID), BF16), v((640, HID), BF16),
         v((3072, HID), BF16), v((3072, HID), BF16), v((HID, 3072), BF16),
         v((HID, NC), F32), v((HID, NC), F32),
@@ -473,17 +560,17 @@
         v((NZ, 3, FD, CB), BF16), v((NZ, 3, FD // 2, CT), BF16),
         v((NZ, FD, CB), BF16), v((NZ, FD // 2, CT), BF16),
         v((4, FD, CB), BF16), v((4, FD, CB), BF16), v((4, FD // 2, CT), BF16), v((4, FD // 2, CT), BF16),
-        dma((5,)),
+        dma((8,)),
         dma((NE,)), dma((NE,)), dma((NE,)), dma((NE,)),
-        dma((NX,)), dma((NX,)), dma((4,)), dma((4,)), dma((4,)), dma((4,)),
+        dma((NX,)), dma((NX,)), dma((4, NX)), dma((4, NX)), dma((4, NX)), dma((4, NX)),
         dma((2, 4)), dma((2, 4)), dma((2, 4)), dma((2, 4)), dma((NZ, 3, 2)), dma((NZ, 3, 2)),
-        dma((4,)), dma((4,)), dma((4,)), dma((4,)), dma((NZ, 3, 2)), dma((NZ, 3, 2)),
+        dma((4, NX)), dma((4, NX)), dma((4, NX)), dma((4, NX)), dma((NZ, 3, 2)), dma((NZ, 3, 2)),
         dma((2, 4)), dma((2, 4)), dma((2, 4)), dma((2, 4)), dma((NX,)), dma((NX,)),
     ]
     return pl.pallas_call(
         kernel,
         out_shape=jax.ShapeDtypeStruct(tokens_grad.shape, BF16),
-        in_specs=[vmem] * 3 + [hbm] * 5,
+        in_specs=[hbm] * 8,
         out_specs=vmem,
         scratch_shapes=scratch,
         compiler_params=pltpu.CompilerParams(

time: 88.9 us -> 82.2 us (0.925)
  Pallas kernels: 87.3 us -> 80.6 us
    pallas_call x1, Pallas kernels: 87.3 us -> 80.6 us  [per_device(): pl.pallas_call(kernel, out_shape=jax.ShapeDtypeStruct(tokens_grad.shape,...]
where the time goes in v2:
time: 82.2 us; the launch traced here: 82.1 us
  Pallas kernels  80.6 us (98%)
  local copies, waits for them, and re-layouts  1.42 us (2%)
    pallas_call x1, Pallas kernels, per_device(): pl.pallas_call(kernel, out_shape=jax.ShapeDtypeStruct(tokens_grad.shape,...  80.6 us

profile of v2, /device:TPU:1, one launch (start us, length us, event | category | flops | bytes accessed | tf_op | source)
XLA Modules:
  0.0 82.1 jit_solution(1596355846136315079)
XLA Ops:
  0.0 80.6 %moe_backward.1 = bf16[192,96]{1,0:T(8,128)(2,1)} custom-call(bf16[192,96]{1,0:T(8,128)(2,1)} %tok_hbm.1, s32[2,192]{1,0:T(2,128)} %bitcast.2, f32[2,192]{1,0:T(2,128)} %bitcast.3, bf16[1,576,512]{2,1,0:T(8,128)(2,1)} %gs_hbm.1, bf16[1,576,512]{2,1,0:T(8,128)(2,1)} %us_hbm.1, bf16[1,3072,512]{2,1,0:T(8,128)(2,1)} %gw_hbm.1, bf16[1,3072,512]{2,1,0:T(8,128)(2,1)} %uw_hbm.1, ...), custom_call_target="tpu_custom_call" | custom-call | tf_op jit(solution)/shard_map/moe_backward/pallas_call | solution.py:570
  80.6 1.4 %copy.10 = bf16[192,96]{1,0:T(8,128)(2,1)} copy(bf16[192,96]{1,0:T(8,128)(2,1)} %moe_backward.1) | data formatting | bytes 73728

commit v3 on v2

--- a/solution.py
+++ b/solution.py
@@ -1,4 +1,4 @@
-import functools
+import math
 
 import jax
 import jax.numpy as jnp
@@ -49,14 +49,10 @@
 def kernel(
     tok_hbm, ids_hbm, wts_hbm, gs_hbm, us_hbm, gw_hbm, uw_hbm, dw_hbm, out_ref,
     tok_ref, ids_ref, wts_ref, gs, us, gw, uw, dw, act_t, dup_t,
-    onehot, place, snd1, rcv1, snd2, rcv2,
-    xa, xb, xt, xtu, h, gg, ug, slot_t,
+    onehot, pos_ref, weight_ref, snd1, rcv1, snd2, rcv2,
+    xa, xb, xt, xtu, h, gg, ug,
     part, sa, sb, st, ra_p, ra_m, rax, sax, rbx, rtx, qb, qt, rbz_p, rbz_m, rtz_p, rtz_m,
-    ld, a1s, a1r, a2s, a2r,
-    axs, axr, azps, azpr, azms, azmr,
-    bzps, bzpr, bzms, bzmr, bxs, bxr,
-    rzps, rzpr, rzms, rzmr, rxs, rxr,
-    qzps, qzpr, qzms, qzmr, qxs, qxr,
+    size_ref, sent, ld, a1r, a2r, axr, azpr, azmr, bzpr, bzmr, bxr, rzpr, rzmr, rxr, qzpr, qzmr, qxr,
 ):
     e = lax.axis_index("expert")
     z = lax.axis_index("row")
@@ -78,15 +74,22 @@
     def xrows(xx, size):
         return pl.ds(pl.multiple_of(xx * size, size), size)
 
-    started = []
-
-    def send(src, dst, ss, rs, to):
+    sent_bytes = [0, 0, 0, 0]
+
+    def send(phase, src, dst, rs, to):
         copy = pltpu.make_async_remote_copy(
-            src_ref=src, dst_ref=dst, send_sem=ss, recv_sem=rs, device_id=to, device_id_type=MESH
+            src_ref=src, dst_ref=dst, send_sem=sent.at[phase], recv_sem=rs, device_id=to, device_id_type=MESH
         )
         copy.start()
-        started.append(copy)
+        sent_bytes[phase] += 2 * math.prod(src.shape)
         return copy
+
+    def wait_bytes(sem, size):
+        whole = size_ref.at[pl.ds(0, size // 512)]
+        pltpu.make_async_copy(whole, whole, sem).wait()
+
+    def got(sem):
+        wait_bytes(sem, 2 * FD * (CB + CT // 2))
 
     bar = pltpu.get_barrier_semaphore()
     partners = [dev(dz=1), dev(dz=-1)] + [dev(dx=r) for r in range(1, NX)]
@@ -120,39 +123,49 @@
     weight = jnp.where(first, wts[0:1, :], jnp.where(second, wts[1:2, :], 0.0))
     earlier = jnp.where(iota((192, 192), 0) < iota((192, 192), 1), 1.0, 0.0).astype(BF16)
     pos = mm(named.astype(BF16), earlier)
-    pos = jnp.where(named > 0.5, pos, -1.0)
+    pos_ref[...] = jnp.where(named > 0.5, pos, -1.0)
+    weight_ref[...] = weight
     j_iota = iota((128, 192), 0).astype(F32)
-    for i in range(NE):
-        oh = jnp.where(pos[i : i + 1, :] == j_iota, 1.0, 0.0).astype(BF16)
-        onehot[128 * i : 128 * i + 128, :] = oh
-        scaled = (tok_t * weight[i : i + 1, :]).astype(BF16)
-        snd1[i] = mm_nt(scaled, oh).astype(BF16)
+    lane = iota((FD, 128), 1)
+    far_first = (4, 3, 5, 2, 6, 1, 7)
+
+    def dispatch(i):
+        oh = jnp.where(pos_ref[pl.ds(i, 1), :] == j_iota, 1.0, 0.0).astype(BF16)
+        onehot[i] = oh
+        scaled = (tok_t * weight_ref[pl.ds(i, 1), :]).astype(BF16)
+        return mm_nt(scaled, oh).astype(BF16)
 
     pl.semaphore_wait(bar, len(partners))
 
     a2a = {}
-    for r in range(1, NE):
+    for r in far_first:
         to = lax.rem(e + r, NE)
-        a2a[r] = send(snd1.at[to], rcv1.at[e], a1s.at[r], a1r.at[r], dev(de=r))
-    rcv1[e] = snd1[e]
-    pj = iota((128, NC), 0)
-    pc = iota((128, NC), 1)
-    for s in range(NE):
-        place[128 * s : 128 * s + 128, :] = jnp.where(
-            (pc == pj + CAP * s) & (pj < CAP), 1.0, 0.0
-        ).astype(BF16)
+        snd1[to] = dispatch(to)
+        a2a[r] = send(0, snd1.at[to], rcv1.at[e], a1r.at[r], dev(de=r))
+    rcv1[e] = dispatch(e)
     gs[576:640, :] = jnp.zeros((64, HID), BF16)
     us[576:640, :] = jnp.zeros((64, HID), BF16)
     h[...] = jnp.zeros_like(h)
-    for r in range(1, NE):
+    for r in far_first:
         a2a[r].wait_recv()
-    rows = mm(rcv1[0], place[0:128, :])
-    for s in range(1, NE):
-        rows += mm(rcv1[s], place[128 * s : 128 * s + 128, :])
-    xa[z, xrows(x, FD), :] = rows[:, :CA].astype(BF16)
-    xb[z, xrows(x, FD), :] = rows[:, CA : CA + CB].astype(BF16)
-    tail = rows[:, CA + CB :]
+    tiles = [jnp.zeros((FD, 128), F32) for _ in range(NC // 128)]
+    for s in range(NE):
+        q, shift = divmod(CAP * s, 128)
+        block = rcv1[s].astype(F32)
+        if shift:
+            block = pltpu.roll(block, shift, 1)
+        if shift + CAP <= 128:
+            tiles[q] += block
+        else:
+            tiles[q] += jnp.where(lane >= shift, block, 0.0)
+            tiles[q + 1] += jnp.where(lane < shift, block, 0.0)
+    tiles = [t.astype(BF16) for t in tiles]
+    xb[z, xrows(x, FD), :128] = tiles[2]
+    xb[z, xrows(x, FD), 128:] = tiles[3]
+    tail = tiles[4].astype(F32)
     xt[z, xrows(x, FD // 2), :] = (tail[: FD // 2] + pltpu.roll(tail[FD // 2 :], 64, 1)).astype(BF16)
+    xa[z, xrows(x, FD), :128] = tiles[0]
+    xa[z, xrows(x, FD), 128:] = tiles[1]
 
     def gelu_block(b):
         def body(c, carry):
@@ -192,24 +205,18 @@
         h[:, CA + CB :] += mm(dw[:, cols], xtu[zz])
 
     def bz(zz, to_plus, k):
-        ss, rs, to = (bzps, bzpr, dev(dz=1)) if to_plus else (bzms, bzmr, dev(dz=-1))
-        m = xb.at[zz, xrows(x, FD)]
-        t = xt.at[zz, xrows(x, FD // 2)]
-        return (send(m, m, ss.at[0, k], rs.at[0, k], to), send(t, t, ss.at[1, k], rs.at[1, k], to))
+        rs, to = (bzpr, dev(dz=1)) if to_plus else (bzmr, dev(dz=-1))
+        for buf, size in ((xb, FD), (xt, FD // 2)):
+            m = buf.at[zz, xrows(x, size)]
+            send(1, m, m, rs.at[k], to)
+        return rs.at[k]
 
     def bx(d, xx, which, dx):
-        i = d % NZ
-        m = xb.at[zrel(d), xrows(xx, FD)]
-        t = xt.at[zrel(d), xrows(xx, FD // 2)]
-        to = dev(dx=dx)
-        return (
-            send(m, m, bxs.at[i, which, 0], bxr.at[i, which, 0], to),
-            send(t, t, bxs.at[i, which, 1], bxr.at[i, which, 1], to),
-        )
-
-    def got(pair):
-        for c in pair:
-            c.wait_recv()
+        sem = bxr.at[d % NZ, which]
+        for buf, size in ((xb, FD), (xt, FD // 2)):
+            m = buf.at[zrel(d), xrows(xx, size)]
+            send(1, m, m, sem, dev(dx=dx))
+        return sem
 
     bzp, bzm, bxc, azp, azm = {}, {}, {}, {}, {}
 
@@ -230,9 +237,9 @@
         got(bxc[d, 2])
 
     def az(zz, j, to_plus, k):
-        ss, rs, to = (azps, azpr, dev(dz=1)) if to_plus else (azms, azmr, dev(dz=-1))
+        rs, to = (azpr, dev(dz=1)) if to_plus else (azmr, dev(dz=-1))
         m = xa.at[zz, xrows(xrel(j), FD)]
-        return send(m, m, ss.at[k, j], rs.at[k, j], to)
+        return send(1, m, m, rs.at[k, j], to)
 
     def ds(k):
         return (k,) if k in (0, 4) else (-k, k)
@@ -245,7 +252,7 @@
     azp[0, 0] = az(z, 0, True, 0)
     azm[0, 0] = az(z, 0, False, 0)
     own = xa.at[z, xrows(x, FD)]
-    ax = {r: send(own, own, axs.at[r], axr.at[r], dev(dx=r)) for r in (1, 3, 2)}
+    ax = {r: send(1, own, own, axr.at[r], dev(dx=r)) for r in (1, 3, 2)}
     bx_first(0)
     for c in loads[:2]:
         c.wait()
@@ -351,25 +358,22 @@
 
     def ra(k, j, to_plus):
         zz = zrel(4 - k) if to_plus else zrel(k - 4)
-        ss, rs, to, rb, kept = (
-            (rzps, rzpr, dev(dz=1), ra_p, rap) if to_plus else (rzms, rzmr, dev(dz=-1), ra_m, ram)
-        )
+        rs, to, rb, kept = (rzpr, dev(dz=1), ra_p, rap) if to_plus else (rzmr, dev(dz=-1), ra_m, ram)
         r = xrows(xrel(j), FD)
         v = part[zz, r, :CA]
         if (k - 1, j) in kept:
             kept[k - 1, j].wait_recv()
             v = v + rb[k - 1, r].astype(F32)
         sa[zz, r] = v.astype(BF16)
-        kept[k, j] = send(sa.at[zz, r], rb.at[k, r], ss.at[k, j], rs.at[k, j], to)
+        kept[k, j] = send(2, sa.at[zz, r], rb.at[k, r], rs.at[k, j], to)
 
     def rx(d, xx, which, dx):
         i = d % NZ
         zz = zrel(d)
-        to = dev(dx=dx)
-        return (
-            send(sb.at[zz, xrows(xx, FD)], rbx.at[i, which], rxs.at[i, which, 0], rxr.at[i, which, 0], to),
-            send(st.at[zz, xrows(xx, FD // 2)], rtx.at[i, which], rxs.at[i, which, 1], rxr.at[i, which, 1], to),
-        )
+        sem = rxr.at[i, which]
+        send(2, sb.at[zz, xrows(xx, FD)], rbx.at[i, which], sem, dev(dx=dx))
+        send(2, st.at[zz, xrows(xx, FD // 2)], rtx.at[i, which], sem, dev(dx=dx))
+        return sem
 
     rxc = {}
 
@@ -411,15 +415,12 @@
         i = (4 - k) % NZ if to_plus else (k - 4) % NZ
         qb[i] = m.astype(BF16)
         qt[i] = t.astype(BF16)
-        ss, rs, to, rb, rt = (
-            (qzps, qzpr, dev(dz=1), rbz_p, rtz_p)
-            if to_plus
-            else (qzms, qzmr, dev(dz=-1), rbz_m, rtz_m)
+        rs, to, rb, rt = (
+            (qzpr, dev(dz=1), rbz_p, rtz_p) if to_plus else (qzmr, dev(dz=-1), rbz_m, rtz_m)
         )
-        qc[k, to_plus] = (
-            send(qb.at[i], rb.at[k], ss.at[0, k], rs.at[0, k], to),
-            send(qt.at[i], rt.at[k], ss.at[1, k], rs.at[1, k], to),
-        )
+        send(2, qb.at[i], rb.at[k], rs.at[k], to)
+        send(2, qt.at[i], rt.at[k], rs.at[k], to)
+        qc[k, to_plus] = rs.at[k]
 
     def q_stage(k):
         if k == 0:
@@ -495,7 +496,7 @@
         v = part[z, r, :CA] + ra_p[3, r].astype(F32) + ra_m[3, r].astype(F32)
         if j:
             sax[r, :] = v.astype(BF16)
-            sx.append(send(sax.at[r], rax.at[j], qxs.at[j], qxr.at[j], dev(dx=j)))
+            sx.append(send(2, sax.at[r], rax.at[j], qxr.at[j], dev(dx=j)))
         else:
             own_a.append(v)
 
@@ -511,32 +512,35 @@
     got(qc[3, False])
     m = m + rbz_p[3].astype(F32) + rbz_m[3].astype(F32)
     t = t + rtz_p[3].astype(F32) + rtz_m[3].astype(F32)
-    slot_t[:, CA : CA + CB] = m.astype(BF16)
     low = iota((FD // 2, 128), 1) < 64
-    slot_t[: FD // 2, CA + CB :] = jnp.where(low, t, 0.0).astype(BF16)
-    slot_t[FD // 2 :, CA + CB :] = jnp.where(low, pltpu.roll(t, 64, 1), 0.0).astype(BF16)
+    t = jnp.concatenate([jnp.where(low, t, 0.0), jnp.where(low, pltpu.roll(t, 64, 1), 0.0)], axis=0)
     a = own_a[0]
     for c in sx:
         c.wait_recv()
     for r in range(1, NX):
         a = a + rax[r].astype(F32)
-    slot_t[:, :CA] = a.astype(BF16)
-
+
+    tiles = [v.astype(BF16).astype(F32) for v in (a[:, :128], a[:, 128:], m[:, :128], m[:, 128:], t)]
     for s in range(NE):
-        snd2[s] = mm_nt(slot_t[...], place[128 * s : 128 * s + 128, :]).astype(BF16)
+        q, shift = divmod(CAP * s, 128)
+        block = tiles[q]
+        if shift + CAP > 128:
+            block = jnp.where(lane >= shift, block, tiles[q + 1])
+        if shift:
+            block = pltpu.roll(block, 128 - shift, 1)
+        snd2[s] = block.astype(BF16)
     back = {}
-    for r in range(1, NE):
+    for r in far_first:
         to = lax.rem(e + r, NE)
-        back[r] = send(snd2.at[to], rcv2.at[e], a2s.at[r], a2r.at[r], dev(de=r))
-    rcv2[e] = snd2[e]
-    for r in range(1, NE):
+        back[r] = send(3, snd2.at[to], rcv2.at[e], a2r.at[r], dev(de=r))
+    o = mm(snd2[e], onehot[e])
+    for r in (1, 7, 2, 6, 3, 5, 4):
         back[r].wait_recv()
-    o = mm(rcv2[0], onehot[0:128, :])
-    for s in range(1, NE):
-        o += mm(rcv2[s], onehot[128 * s : 128 * s + 128, :])
+        i = lax.rem(e + NE - r, NE)
+        o += mm(rcv2[i], onehot[i])
     out_ref[...] = o.T.astype(BF16)
-    for c in started:
-        c.wait_send()
+    for phase, size in enumerate(sent_bytes):
+        wait_bytes(sent.at[phase], size)
 
 
 def per_device(tokens_grad, expert_ids, combine_weights, gate_saved, up_saved, gate_weight, up_weight, down_weight):
@@ -549,10 +553,10 @@
         v((640, HID), BF16), v((640, HID), BF16),
         v((3072, HID), BF16), v((3072, HID), BF16), v((HID, 3072), BF16),
         v((HID, NC), F32), v((HID, NC), F32),
-        v((1024, 192), BF16), v((1024, NC), BF16),
+        v((NE, 128, 192), BF16), v((NE, 192), F32), v((NE, 192), F32),
         v((NE, FD, 128), BF16), v((NE, FD, 128), BF16), v((NE, FD, 128), BF16), v((NE, FD, 128), BF16),
         v((NZ, SLAB, CA), BF16), v((NZ, SLAB, CB), BF16), v((NZ, HALF, CT), BF16), v((NZ, SLAB, CT), BF16),
-        v((HID, NC), F32), v((HID, NC), BF16), v((HID, NC), BF16), v((FD, NC), BF16),
+        v((HID, NC), F32), v((HID, NC), BF16), v((HID, NC), BF16),
         v((NZ, SLAB, NC), F32),
         v((NZ, SLAB, CA), BF16), v((NZ, SLAB, CB), BF16), v((NZ, HALF, CT), BF16),
         v((4, SLAB, CA), BF16), v((4, SLAB, CA), BF16),
@@ -560,12 +564,10 @@
         v((NZ, 3, FD, CB), BF16), v((NZ, 3, FD // 2, CT), BF16),
         v((NZ, FD, CB), BF16), v((NZ, FD // 2, CT), BF16),
         v((4, FD, CB), BF16), v((4, FD, CB), BF16), v((4, FD // 2, CT), BF16), v((4, FD // 2, CT), BF16),
-        dma((8,)),
-        dma((NE,)), dma((NE,)), dma((NE,)), dma((NE,)),
-        dma((NX,)), dma((NX,)), dma((4, NX)), dma((4, NX)), dma((4, NX)), dma((4, NX)),
-        dma((2, 4)), dma((2, 4)), dma((2, 4)), dma((2, 4)), dma((NZ, 3, 2)), dma((NZ, 3, 2)),
-        dma((4, NX)), dma((4, NX)), dma((4, NX)), dma((4, NX)), dma((NZ, 3, 2)), dma((NZ, 3, 2)),
-        dma((2, 4)), dma((2, 4)), dma((2, 4)), dma((2, 4)), dma((NX,)), dma((NX,)),
+        v((6720, 128), F32),
+        dma((4,)), dma((8,)), dma((NE,)), dma((NE,)),
+        dma((NX,)), dma((4, NX)), dma((4, NX)), dma((4,)), dma((3,)), dma((NZ, 3)),
+        dma((4, NX)), dma((4, NX)), dma((NZ, 3)), dma((4,)), dma((4,)), dma((NX,)),
     ]
     return pl.pallas_call(
         kernel,

time: 82.2 us -> 78.2 us (0.951)
  Pallas kernels: 80.6 us -> 76.7 us
    pallas_call x1, Pallas kernels: 80.6 us -> 76.7 us  [per_device(): pl.pallas_call(kernel, out_shape=jax.ShapeDtypeStruct(tokens_grad.shape,...]
where the time goes in v3:
time: 78.2 us; the launch traced here: 78.1 us
  Pallas kernels  76.7 us (98%)
  local copies, waits for them, and re-layouts  1.42 us (2%)
    pallas_call x1, Pallas kernels, per_device(): pl.pallas_call(kernel, out_shape=jax.ShapeDtypeStruct(tokens_grad.shape,...  76.7 us

profile of v3, /device:TPU:1, one launch (start us, length us, event | category | flops | bytes accessed | tf_op | source)
XLA Modules:
  0.0 78.1 jit_solution(13784165315621873966)
XLA Ops:
  0.0 76.7 %moe_backward.1 = bf16[192,96]{1,0:T(8,128)(2,1)} custom-call(bf16[192,96]{1,0:T(8,128)(2,1)} %tok_hbm.1, s32[2,192]{1,0:T(2,128)} %bitcast.2, f32[2,192]{1,0:T(2,128)} %bitcast.3, bf16[1,576,512]{2,1,0:T(8,128)(2,1)} %gs_hbm.1, bf16[1,576,512]{2,1,0:T(8,128)(2,1)} %us_hbm.1, bf16[1,3072,512]{2,1,0:T(8,128)(2,1)} %gw_hbm.1, bf16[1,3072,512]{2,1,0:T(8,128)(2,1)} %uw_hbm.1, ...), custom_call_target="tpu_custom_call" | custom-call | tf_op jit(solution)/shard_map/moe_backward/pallas_call | solution.py:572
  76.7 1.4 %copy.10 = bf16[192,96]{1,0:T(8,128)(2,1)} copy(bf16[192,96]{1,0:T(8,128)(2,1)} %moe_backward.1) | data formatting | bytes 73728

commit v4 on v3

--- a/solution.py
+++ b/solution.py
@@ -223,8 +223,12 @@
     def bx_first(d):
         bxc[d, 0] = bx(d, x, 0, 1)
         bxc[d, 1] = bx(d, x, 1, -1)
+        if d == 4:
+            bxc[d, 2] = bx(d, x, 2, 2)
 
     def bx_second(d):
+        if d == 4:
+            return
         if d % 2 == 0:
             got(bxc[d, 0])
             bxc[d, 2] = bx(d, xrel(-1), 2, 1)
@@ -233,6 +237,8 @@
             bxc[d, 2] = bx(d, xrel(1), 2, -1)
 
     def bx_done(d):
+        if d == 4:
+            got(bxc[d, 0])
         got(bxc[d, 1 if d % 2 == 0 else 0])
         got(bxc[d, 2])
 
@@ -293,41 +299,42 @@
         azm[0, j] = az(z, j, False, 0)
     b_step(1)
     second(0)
-    gelu_block(0)
     a_step(1, 0)
+    b_step(2)
     loads[2].wait()
     both(0, mm_a)
-    b_step(2)
     a_step(1, 1)
-    gelu_block(1)
+    gelu_block(0)
     a_step(1, 2)
     second(1)
+    b_step(3)
     a_step(1, 3)
+    gelu_block(1)
+    both(1, mm_a)
     a_step(2, 0)
     done(0)
-    b_step(3)
-    both(1, mm_a)
     a_step(2, 1)
+    second(2)
+    a_step(2, 2)
+    b_step(4)
     gelu_block(2)
-    a_step(2, 2)
-    second(2)
     a_step(2, 3)
     done(1)
-    b_step(4)
     a_step(3, 0)
     both(2, mm_a)
+    second(3)
     a_step(3, 1)
     gelu_block(3)
     a_step(3, 2)
-    second(3)
     a_step(3, 3)
     done(2)
     gelu_block(4)
     both(3, mm_a)
     a_step(4, 0)
-    second(4)
+    done(3)
     a_step(4, 1)
     both(4, mm_a)
+    done(4)
 
     def hidden(cols):
         hh = h[:, cols]
@@ -379,8 +386,10 @@
 
     def rx_first(d):
         s = 1 if d % 2 == 0 else -1
-        rxc[d, 0] = rx(d, xrel(2), 0, s)
+        rxc[d, 0] = rx(d, xrel(2), 0, 2 if d == 0 else s)
         rxc[d, 1] = rx(d, xrel(-s), 1, -s)
+        if d == 0:
+            rxc[d, 2] = rx(d, xrel(s), 2, s)
 
     def tail_of(zz, xx):
         base = pl.multiple_of(xx * FD, FD // 2)
@@ -389,6 +398,8 @@
         return top + pltpu.roll(bot, 64, 1)
 
     def rx_second(d):
+        if d == 0:
+            return
         s = 1 if d % 2 == 0 else -1
         i = d % NZ
         zz = zrel(d)
@@ -407,6 +418,10 @@
         got(rxc[d, 2])
         m = part[zz, xrows(x, FD), CA : CA + CB] + rbx[i, 1].astype(F32) + rbx[i, 2].astype(F32)
         t = tail_of(zz, x) + rtx[i, 1].astype(F32) + rtx[i, 2].astype(F32)
+        if d == 0:
+            got(rxc[d, 0])
+            m = m + rbx[i, 0].astype(F32)
+            t = t + rtx[i, 0].astype(F32)
         return m, t
 
     qc = {}
@@ -453,39 +468,6 @@
         for d in ds(k):
             rx_second(d)
 
-    both(4, mm_pa)
-    ra_both(0, 0)
-    ra_both(0, 1)
-    done(3)
-    both(3, mm_pa)
-    ra_both(1, 0)
-    ra_both(1, 1)
-    done(4)
-    hidden(slice(CA, NC))
-    firsts(4)
-    ra_both(1, 2)
-    ra_both(1, 3)
-    firsts(3)
-    both(2, mm_pa)
-    ra_both(2, 0)
-    seconds(4)
-    ra_both(2, 1)
-    firsts(2)
-    seconds(3)
-    ra_both(2, 2)
-    ra_both(2, 3)
-    q_stage(0)
-    both(1, mm_pa)
-    ra_both(3, 0)
-    firsts(1)
-    seconds(2)
-    ra_both(3, 1)
-    ra_both(3, 2)
-    q_stage(1)
-    firsts(0)
-    ra_both(3, 3)
-    both(0, mm_pa)
-    seconds(1)
     sx = []
     own_a = []
 
@@ -500,12 +482,42 @@
         else:
             own_a.append(v)
 
+    both(4, mm_pa)
+    ra_both(0, 0)
+    ra_both(0, 1)
+    hidden(slice(CA, NC))
+    firsts(4)
+    both(3, mm_pa)
+    ra_both(1, 0)
+    ra_both(1, 1)
+    firsts(3)
+    ra_both(1, 2)
+    ra_both(1, 3)
+    seconds(4)
+    both(2, mm_pa)
+    firsts(2)
+    ra_both(2, 0)
+    ra_both(2, 1)
+    seconds(3)
+    q_stage(0)
+    ra_both(2, 2)
+    firsts(1)
+    ra_both(2, 3)
+    both(1, mm_pa)
+    seconds(2)
+    q_stage(1)
+    ra_both(3, 0)
+    firsts(0)
+    ra_both(3, 1)
+    seconds(1)
+    q_stage(2)
+    ra_both(3, 2)
+    ra_both(3, 3)
+    both(0, mm_pa)
     final_a(2)
-    q_stage(2)
+    q_stage(3)
     final_a(3)
-    seconds(0)
     final_a(1)
-    q_stage(3)
     final_a(0)
     m, t = rx_done(0)
     got(qc[3, True])
@@ -571,7 +583,7 @@
     ]
     return pl.pallas_call(
         kernel,
-        out_shape=jax.ShapeDtypeStruct(tokens_grad.shape, BF16),
+        out_shape=pltpu.VMEM(tokens_grad.shape, BF16),
         in_specs=[hbm] * 8,
         out_specs=vmem,
         scratch_shapes=scratch,

time: 78.2 us -> 75.9 us (0.971)
  Pallas kernels: 76.7 us -> 75.2 us
  local copies, waits for them, and re-layouts: 1.42 us -> 0.62 us
    pallas_call x1, Pallas kernels: 76.7 us -> 75.2 us  [per_device(): pl.pallas_call(kernel, out_shape=pltpu.VMEM(tokens_grad.shape, BF16), in_...]
    unnamed x1, local copies, waits for them, and re-layouts: 1.42 us -> 0.62 us
where the time goes in v4:
time: 75.9 us; the launch traced here: 75.8 us
  Pallas kernels  75.2 us (99%)
    pallas_call x1, Pallas kernels, per_device(): pl.pallas_call(kernel, out_shape=pltpu.VMEM(tokens_grad.shape, BF16), in_...  75.2 us

profile of v4, /device:TPU:1, one launch (start us, length us, event | category | flops | bytes accessed | tf_op | source)
XLA Modules:
  0.0 75.8 jit_solution(16245226398776486374)
XLA Ops:
  0.0 75.2 %moe_backward.1 = bf16[192,96]{1,0:T(8,128)(2,1)S(1)} custom-call(bf16[192,96]{1,0:T(8,128)(2,1)} %tok_hbm.1, s32[2,192]{1,0:T(2,128)} %bitcast.2, f32[2,192]{1,0:T(2,128)} %bitcast.3, bf16[1,576,512]{2,1,0:T(8,128)(2,1)} %gs_hbm.1, bf16[1,576,512]{2,1,0:T(8,128)(2,1)} %us_hbm.1, bf16[1,3072,512]{2,1,0:T(8,128)(2,1)} %gw_hbm.1, ...), custom_call_target="tpu_custom_call" | custom-call | tf_op jit(solution)/shard_map/moe_backward/pallas_call | solution.py:584
  75.2 0.6 copy.10

commit v5 on v4

--- a/solution.py
+++ b/solution.py
@@ -44,6 +44,31 @@
 
 def iota(shape, dim):
     return lax.broadcasted_iota(jnp.int32, shape, dim)
+
+
+def pack(block):
+    half, rows = FD // 2, 16
+    lane = iota((half, 128), 1)
+    top = jnp.where(lane < 64, block[:half], pltpu.roll(block[half:], 64, 1))
+    lane = iota((rows, 128), 1)
+    rest = jnp.zeros((rows, 128), F32)
+    for g in range(FD // rows):
+        moved = pltpu.roll(block[rows * g : rows * g + rows], (64 + 8 * g) % 128, 1)
+        rest += jnp.where((lane >= 8 * g) & (lane < 8 * g + 8), moved, 0.0)
+    return jnp.concatenate([top, rest], axis=0).astype(BF16)
+
+
+def unpack(packed):
+    half, rows = FD // 2, 16
+    packed = packed.astype(F32)
+    lane = iota((rows, 128), 1)
+    top, rest = packed[:half], packed[half:]
+    both = jnp.concatenate([top, pltpu.roll(top, 64, 1)], axis=0)
+    moved = jnp.concatenate(
+        [pltpu.roll(rest, (64 - 8 * g) % 128, 1) for g in range(FD // rows)], axis=0
+    )
+    lane = iota((FD, 128), 1)
+    return jnp.where(lane < 64, both, jnp.where(lane < CAP, moved, 0.0))
 
 
 def kernel(
@@ -133,25 +158,25 @@
         oh = jnp.where(pos_ref[pl.ds(i, 1), :] == j_iota, 1.0, 0.0).astype(BF16)
         onehot[i] = oh
         scaled = (tok_t * weight_ref[pl.ds(i, 1), :]).astype(BF16)
-        return mm_nt(scaled, oh).astype(BF16)
-
+        return pack(mm_nt(scaled, oh))
+
+    blocks = [dispatch(i) for i in range(NE)]
+    for i in range(NE):
+        snd1[i] = blocks[i]
     pl.semaphore_wait(bar, len(partners))
 
-    a2a = {}
     for r in far_first:
         to = lax.rem(e + r, NE)
-        snd1[to] = dispatch(to)
-        a2a[r] = send(0, snd1.at[to], rcv1.at[e], a1r.at[r], dev(de=r))
-    rcv1[e] = dispatch(e)
+        send(0, snd1.at[to], rcv1.at[e], a1r.at[0], dev(de=r))
+    rcv1[e] = snd1[e]
     gs[576:640, :] = jnp.zeros((64, HID), BF16)
     us[576:640, :] = jnp.zeros((64, HID), BF16)
     h[...] = jnp.zeros_like(h)
-    for r in far_first:
-        a2a[r].wait_recv()
+    wait_bytes(a1r.at[0], (NE - 1) * 64 * 128 * 2)
     tiles = [jnp.zeros((FD, 128), F32) for _ in range(NC // 128)]
     for s in range(NE):
         q, shift = divmod(CAP * s, 128)
-        block = rcv1[s].astype(F32)
+        block = unpack(rcv1[s])
         if shift:
             block = pltpu.roll(block, shift, 1)
         if shift + CAP <= 128:
@@ -468,7 +493,6 @@
         for d in ds(k):
             rx_second(d)
 
-    sx = []
     own_a = []
 
     def final_a(j):
@@ -478,7 +502,7 @@
         v = part[z, r, :CA] + ra_p[3, r].astype(F32) + ra_m[3, r].astype(F32)
         if j:
             sax[r, :] = v.astype(BF16)
-            sx.append(send(2, sax.at[r], rax.at[j], qxr.at[j], dev(dx=j)))
+            send(2, sax.at[r], rax.at[j], qxr.at[0], dev(dx=j))
         else:
             own_a.append(v)
 
@@ -527,8 +551,7 @@
     low = iota((FD // 2, 128), 1) < 64
     t = jnp.concatenate([jnp.where(low, t, 0.0), jnp.where(low, pltpu.roll(t, 64, 1), 0.0)], axis=0)
     a = own_a[0]
-    for c in sx:
-        c.wait_recv()
+    wait_bytes(qxr.at[0], (NX - 1) * FD * CA * 2)
     for r in range(1, NX):
         a = a + rax[r].astype(F32)
 
@@ -540,16 +563,15 @@
             block = jnp.where(lane >= shift, block, tiles[q + 1])
         if shift:
             block = pltpu.roll(block, 128 - shift, 1)
-        snd2[s] = block.astype(BF16)
-    back = {}
+        snd2[s] = pack(block)
     for r in far_first:
         to = lax.rem(e + r, NE)
-        back[r] = send(3, snd2.at[to], rcv2.at[e], a2r.at[r], dev(de=r))
-    o = mm(snd2[e], onehot[e])
+        send(3, snd2.at[to], rcv2.at[e], a2r.at[0], dev(de=r))
+    o = mm(unpack(snd2[e]).astype(BF16), onehot[e])
+    wait_bytes(a2r.at[0], (NE - 1) * 64 * 128 * 2)
     for r in (1, 7, 2, 6, 3, 5, 4):
-        back[r].wait_recv()
         i = lax.rem(e + NE - r, NE)
-        o += mm(rcv2[i], onehot[i])
+        o += mm(unpack(rcv2[i]).astype(BF16), onehot[i])
     out_ref[...] = o.T.astype(BF16)
     for phase, size in enumerate(sent_bytes):
         wait_bytes(sent.at[phase], size)
@@ -566,7 +588,7 @@
         v((3072, HID), BF16), v((3072, HID), BF16), v((HID, 3072), BF16),
         v((HID, NC), F32), v((HID, NC), F32),
         v((NE, 128, 192), BF16), v((NE, 192), F32), v((NE, 192), F32),
-        v((NE, FD, 128), BF16), v((NE, FD, 128), BF16), v((NE, FD, 128), BF16), v((NE, FD, 128), BF16),
+        v((NE, 64, 128), BF16), v((NE, 64, 128), BF16), v((NE, 64, 128), BF16), v((NE, 64, 128), BF16),
         v((NZ, SLAB, CA), BF16), v((NZ, SLAB, CB), BF16), v((NZ, HALF, CT), BF16), v((NZ, SLAB, CT), BF16),
         v((HID, NC), F32), v((HID, NC), BF16), v((HID, NC), BF16),
         v((NZ, SLAB, NC), F32),
@@ -577,9 +599,9 @@
         v((NZ, FD, CB), BF16), v((NZ, FD // 2, CT), BF16),
         v((4, FD, CB), BF16), v((4, FD, CB), BF16), v((4, FD // 2, CT), BF16), v((4, FD // 2, CT), BF16),
         v((6720, 128), F32),
-        dma((4,)), dma((8,)), dma((NE,)), dma((NE,)),
+        dma((4,)), dma((8,)), dma((1,)), dma((1,)),
         dma((NX,)), dma((4, NX)), dma((4, NX)), dma((4,)), dma((3,)), dma((NZ, 3)),
-        dma((4, NX)), dma((4, NX)), dma((NZ, 3)), dma((4,)), dma((4,)), dma((NX,)),
+        dma((4, NX)), dma((4, NX)), dma((NZ, 3)), dma((4,)), dma((4,)), dma((1,)),
     ]
     return pl.pallas_call(
         kernel,

time: 75.9 us -> 75.4 us (level)
  no operation moved by 1% of the time
where the time goes in v5:
time: 75.4 us; the launch traced here: 75.3 us
  Pallas kernels  74.7 us (99%)
    pallas_call x1, Pallas kernels, per_device(): pl.pallas_call(kernel, out_shape=pltpu.VMEM(tokens_grad.shape, BF16), in_...  74.7 us

profile of v5, /device:TPU:1, one launch (start us, length us, event | category | flops | bytes accessed | tf_op | source)
XLA Modules:
  0.0 75.3 jit_solution(4142587865218851738)
XLA Ops:
  0.0 74.7 %moe_backward.1 = bf16[192,96]{1,0:T(8,128)(2,1)S(1)} custom-call(bf16[192,96]{1,0:T(8,128)(2,1)} %tok_hbm.1, s32[2,192]{1,0:T(2,128)} %bitcast.2, f32[2,192]{1,0:T(2,128)} %bitcast.3, bf16[1,576,512]{2,1,0:T(8,128)(2,1)} %gs_hbm.1, bf16[1,576,512]{2,1,0:T(8,128)(2,1)} %us_hbm.1, bf16[1,3072,512]{2,1,0:T(8,128)(2,1)} %gw_hbm.1, ...), custom_call_target="tpu_custom_call" | custom-call | tf_op jit(solution)/shard_map/moe_backward/pallas_call | solution.py:606
  74.7 0.6 copy.10

commit v6 on v5

--- a/solution.py
+++ b/solution.py
@@ -172,6 +172,21 @@
     gs[576:640, :] = jnp.zeros((64, HID), BF16)
     us[576:640, :] = jnp.zeros((64, HID), BF16)
     h[...] = jnp.zeros_like(h)
+    def gelu_block(b):
+        def body(c, carry):
+            cols = pl.ds(pl.multiple_of(c * 128, 128), 128)
+            act, der = gelu_pair(gs[128 * b : 128 * b + 128, cols].astype(F32))
+            der = der * us[128 * b : 128 * b + 128, cols].astype(F32)
+            act_t[cols, 128 * b : 128 * b + 128] = act.T
+            dup_t[cols, 128 * b : 128 * b + 128] = der.T
+            return carry
+
+        lax.fori_loop(0, HID // 128, body, 0)
+
+    for c in loads[:2]:
+        c.wait()
+    for b in range(5):
+        gelu_block(b)
     wait_bytes(a1r.at[0], (NE - 1) * 64 * 128 * 2)
     tiles = [jnp.zeros((FD, 128), F32) for _ in range(NC // 128)]
     for s in range(NE):
@@ -192,17 +207,6 @@
     xa[z, xrows(x, FD), :128] = tiles[0]
     xa[z, xrows(x, FD), 128:] = tiles[1]
 
-    def gelu_block(b):
-        def body(c, carry):
-            cols = pl.ds(pl.multiple_of(c * 128, 128), 128)
-            act, der = gelu_pair(gs[128 * b : 128 * b + 128, cols].astype(F32))
-            der = der * us[128 * b : 128 * b + 128, cols].astype(F32)
-            act_t[cols, 128 * b : 128 * b + 128] = act.T
-            dup_t[cols, 128 * b : 128 * b + 128] = der.T
-            return carry
-
-        lax.fori_loop(0, HID // 128, body, 0)
-
     def both(k, body):
         if k in (0, 4):
             body(zrel(k))
@@ -285,8 +289,6 @@
     own = xa.at[z, xrows(x, FD)]
     ax = {r: send(1, own, own, axr.at[r], dev(dx=r)) for r in (1, 3, 2)}
     bx_first(0)
-    for c in loads[:2]:
-        c.wait()
 
     def b_step(k):
         got(bzp[k - 1])
@@ -329,12 +331,10 @@
     loads[2].wait()
     both(0, mm_a)
     a_step(1, 1)
-    gelu_block(0)
     a_step(1, 2)
     second(1)
     b_step(3)
     a_step(1, 3)
-    gelu_block(1)
     both(1, mm_a)
     a_step(2, 0)
     done(0)
@@ -342,18 +342,15 @@
     second(2)
     a_step(2, 2)
     b_step(4)
-    gelu_block(2)
     a_step(2, 3)
     done(1)
     a_step(3, 0)
     both(2, mm_a)
     second(3)
     a_step(3, 1)
-    gelu_block(3)
     a_step(3, 2)
     a_step(3, 3)
     done(2)
-    gelu_block(4)
     both(3, mm_a)
     a_step(4, 0)
     done(3)

time: 75.4 us -> 75 us (level)
  no operation moved by 1% of the time
where the time goes in v6:
time: 75 us; the launch traced here: 74.9 us
  Pallas kernels  74.3 us (99%)
    pallas_call x1, Pallas kernels, per_device(): pl.pallas_call(kernel, out_shape=pltpu.VMEM(tokens_grad.shape, BF16), in_...  74.3 us

profile of v6, /device:TPU:1, one launch (start us, length us, event | category | flops | bytes accessed | tf_op | source)
XLA Modules:
  0.0 74.9 jit_solution(10481215732308028916)
XLA Ops:
  0.0 74.3 %moe_backward.1 = bf16[192,96]{1,0:T(8,128)(2,1)S(1)} custom-call(bf16[192,96]{1,0:T(8,128)(2,1)} %tok_hbm.1, s32[2,192]{1,0:T(2,128)} %bitcast.2, f32[2,192]{1,0:T(2,128)} %bitcast.3, bf16[1,576,512]{2,1,0:T(8,128)(2,1)} %gs_hbm.1, bf16[1,576,512]{2,1,0:T(8,128)(2,1)} %us_hbm.1, bf16[1,3072,512]{2,1,0:T(8,128)(2,1)} %gw_hbm.1, ...), custom_call_target="tpu_custom_call" | custom-call | tf_op jit(solution)/shard_map/moe_backward/pallas_call | solution.py:603
  74.3 0.6 copy.10
